TPU v7x, 32 devices: a whole 2x2x4 slice. The times are simulated.
32 devices in a mesh: dp: 8 (over z, x), mp: 4 (over y, core).
Axes of the slice: x: 2, y: 2, z: 4, core: 2. Of those that a mesh axis runs over, the one named last changes fastest.
Arguments:
- patches: bfloat16 [64, 206, 768], P(('dp', 'mp')), may hold values from -9 to 9
- lengths: int32 [64], P(('dp', 'mp')), may hold values from 98 to 197, as said below
- tasks: int32 [64, 1], P(('dp', 'mp')), may hold values from 0 to 7
- prompt_master: float32 [8, 38400], P(None, ('dp', 'mp')), may hold values from -6 to 6
- first_moment: float32 [8, 38400], P(None, ('dp', 'mp')), may hold values from -0.0029296875 to 0.0029296875
- second_moment: float32 [8, 38400], P(None, ('dp', 'mp')), may hold values from 3.2552083e-09 to 1.3020833e-08
- gain_one: float32 [768], replicated, may hold values from 0.1 to 1.9
- gain_two: float32 [768], replicated, may hold values from 0.1 to 1.9
- w_qkv: bfloat16 [768, 3, 768], P('dp', None, 'mp'), may hold values from -0.21875 to 0.21875
- w_out: bfloat16 [768, 768], P('mp', 'dp'), may hold values from -0.875 to 0.875
- w_up: bfloat16 [768, 3072], P('dp', 'mp'), may hold values from -0.21875 to 0.21875
- w_down: bfloat16 [3072, 768], P('mp', 'dp'), may hold values from -0.109375 to 0.109375
- cotangent: bfloat16 [64, 256, 768], P('dp'), may hold values from -7.5 to 7.5
Outputs:
- block_out: bfloat16 [64, 256, 768], P(('dp', 'mp'))
- patch_grad: bfloat16 [64, 206, 768], P(('dp', 'mp'))
- prompt_grad: float32 [8, 38400], P(None, ('dp', 'mp'))
- grad_norm: float32 [], replicated
- new_first: float32 [8, 38400], P(None, ('dp', 'mp'))
- new_second: float32 [8, 38400], P(None, ('dp', 'mp'))
- new_master: float32 [8, 38400], P(None, ('dp', 'mp'))
- new_copy: bfloat16 [8, 38400], P(None, ('dp', 'mp'))
- rms_stats: float32 [3], replicated
Inputs may be any that keep to these rules, and one draw needn't show every extreme that they name: `lengths`: some image has 197 valid patch rows. `tasks`: every prompt set is used by some image.
All inputs are finite; a program needn't handle non-finite values.
Results may differ from a plain program's by a relative error of at most 0.017.
Values may be sent and summed in bfloat16 or wider, within the bound.
A program may use at most 128 MiB of HBM per device.

v0:
```python
import math

import jax
import jax.numpy as jnp
from jax import lax
from jax.sharding import PartitionSpec as P

HEAD_DIM = 64
STEP = 10


eps_norm = 1e-06
clip_level = 1.0
beta_one = 0.9
beta_two = 0.999
learn_rate = 3.0
decay_rate = 0.05
adam_eps = 1e-08


def layer_norm(values, gain):
    centre = jnp.mean(values, axis=-1, keepdims=True)
    shifted = values - centre
    spread = jnp.mean(shifted * shifted, axis=-1, keepdims=True)
    return shifted * lax.rsqrt(spread + eps_norm) * gain


def norm_back(values, gain, upstream):
    centre = jnp.mean(values, axis=-1, keepdims=True)
    shifted = values - centre
    spread = jnp.mean(shifted * shifted, axis=-1, keepdims=True)
    scaled = lax.rsqrt(spread + eps_norm)
    normal_part = shifted * scaled
    weighted = upstream * gain
    return scaled * (
        weighted
        - jnp.mean(weighted, axis=-1, keepdims=True)
        - normal_part * jnp.mean(weighted * normal_part, axis=-1, keepdims=True)
    )


def gelu_slope(upward):
    cumul = 0.5 * (1.0 + lax.erf(upward * 0.7071067811865476))
    density = jnp.exp(-0.5 * upward * upward) * 0.3989422804014327
    return cumul + upward * density


def attend_forward(group_normed, group_limit, w_mix, block_images):
    group_size, row_count, feature_count = group_normed.shape
    lane_width = w_mix.shape[2]
    head_count = lane_width // HEAD_DIM
    scale = 1.0 / math.sqrt(HEAD_DIM)
    mask_all = jnp.arange(row_count, dtype=jnp.int32)[None, :] < group_limit[:, None]

    def one_block(block_index):
        first_row = block_index * block_images
        block_in = lax.dynamic_slice_in_dim(group_normed, first_row, block_images, 0)
        key_mask = lax.dynamic_slice_in_dim(mask_all, first_row, block_images, 0)
        mixed_qkv = jnp.einsum(
            "brd,dce->brce", block_in, w_mix, preferred_element_type=jnp.float32
        ).astype(jnp.bfloat16)
        split_heads = mixed_qkv.reshape(block_images, row_count, 3, head_count, HEAD_DIM)
        scores = (
            jnp.einsum(
                "bqhe,bkhe->bhqk",
                split_heads[:, :, 0],
                split_heads[:, :, 1],
                preferred_element_type=jnp.float32,
            )
            * scale
        )
        scores = jnp.where(key_mask[:, None, None, :], scores, -1e30)
        row_top = jnp.max(scores, axis=-1, keepdims=True)
        exponent = jnp.exp(scores - row_top)
        row_total = jnp.sum(exponent, axis=-1, keepdims=True)
        attend_weights = (exponent / row_total).astype(jnp.bfloat16)
        context = jnp.einsum(
            "bhqk,bkhe->bqhe",
            attend_weights,
            split_heads[:, :, 2],
            preferred_element_type=jnp.float32,
        )
        context = context.astype(jnp.bfloat16).reshape(block_images, row_count, lane_width)
        return (mixed_qkv, context, (row_top + jnp.log(row_total))[..., 0])

    mixed_qkv, context, logsums = lax.map(
        one_block, jnp.arange(group_size // block_images, dtype=jnp.int32)
    )
    return (
        mixed_qkv.reshape(group_size, row_count, 3, lane_width),
        context.reshape(group_size, row_count, lane_width),
        logsums.reshape(group_size, head_count, row_count),
    )


def attend_back(mixed_qkv, logsums, group_limit, grad_context, block_images):
    group_size, row_count, three_parts, lane_width = mixed_qkv.shape
    head_count = lane_width // HEAD_DIM
    scale = 1.0 / math.sqrt(HEAD_DIM)
    mask_all = jnp.arange(row_count, dtype=jnp.int32)[None, :] < group_limit[:, None]

    def one_block(block_index):
        first_row = block_index * block_images
        split_heads = lax.dynamic_slice_in_dim(mixed_qkv, first_row, block_images, 0).reshape(
            block_images, row_count, 3, head_count, HEAD_DIM
        )
        queries = split_heads[:, :, 0]
        keys_all = split_heads[:, :, 1]
        values = split_heads[:, :, 2]
        key_mask = lax.dynamic_slice_in_dim(mask_all, first_row, block_images, 0)
        logsum = lax.dynamic_slice_in_dim(logsums, first_row, block_images, 0)
        grad_out = lax.dynamic_slice_in_dim(grad_context, first_row, block_images, 0).reshape(
            block_images, row_count, head_count, HEAD_DIM
        )
        scores = (
            jnp.einsum("bqhe,bkhe->bhqk", queries, keys_all, preferred_element_type=jnp.float32)
            * scale
        )
        scores = jnp.where(key_mask[:, None, None, :], scores, -1e30)
        attend_weights = jnp.exp(scores - logsum[..., None])
        grad_weights = jnp.einsum(
            "bqhe,bkhe->bhqk", grad_out, values, preferred_element_type=jnp.float32
        )
        row_inner = jnp.sum(attend_weights * grad_weights, axis=-1, keepdims=True)
        grad_scores = (attend_weights * (grad_weights - row_inner)).astype(jnp.bfloat16)
        grad_query = (
            jnp.einsum("bhqk,bkhe->bqhe", grad_scores, keys_all, preferred_element_type=jnp.float32)
            * scale
        )
        grad_key = (
            jnp.einsum("bhqk,bqhe->bkhe", grad_scores, queries, preferred_element_type=jnp.float32)
            * scale
        )
        grad_value = jnp.einsum(
            "bhqk,bqhe->bkhe",
            attend_weights.astype(jnp.bfloat16),
            grad_out,
            preferred_element_type=jnp.float32,
        )
        stacked = jnp.stack([grad_query, grad_key, grad_value], axis=2).astype(jnp.bfloat16)
        return stacked.reshape(block_images, row_count, 3, lane_width)

    grad_mixed = lax.map(one_block, jnp.arange(group_size // block_images, dtype=jnp.int32))
    return grad_mixed.reshape(group_size, row_count, 3, lane_width)


def expand_units(group_two, w_expand, block_images):
    group_size, row_count, feature_count = group_two.shape

    def one_block(block_index):
        block_in = lax.dynamic_slice_in_dim(group_two, block_index * block_images, block_images, 0)
        upward = jnp.einsum("brd,df->brf", block_in, w_expand, preferred_element_type=jnp.float32)
        return jax.nn.gelu(upward, approximate=False).astype(jnp.bfloat16)

    act_units = lax.map(one_block, jnp.arange(group_size // block_images, dtype=jnp.int32))
    return act_units.reshape(group_size, row_count, w_expand.shape[1])


def units_back(grad_group, group_two, w_expand, w_reduce, block_images):
    group_size, row_count, feature_count = group_two.shape

    def one_block(block_index):
        first_row = block_index * block_images
        grad_in = lax.dynamic_slice_in_dim(grad_group, first_row, block_images, 0)
        norm_in = lax.dynamic_slice_in_dim(group_two, first_row, block_images, 0)
        back_units = jnp.einsum(
            "brd,fd->brf", grad_in, w_reduce, preferred_element_type=jnp.float32
        )
        upward = jnp.einsum("brd,df->brf", norm_in, w_expand, preferred_element_type=jnp.float32)
        return (back_units * gelu_slope(upward)).astype(jnp.bfloat16)

    grad_units = lax.map(one_block, jnp.arange(group_size // block_images, dtype=jnp.int32))
    return grad_units.reshape(group_size, row_count, w_expand.shape[1])


def rows_term(source, weight, form):
    return jnp.einsum(form, source, weight, preferred_element_type=jnp.float32)


def body(
    patches,
    lengths,
    tasks,
    prompt_master,
    first_moment,
    second_moment,
    gain_one,
    gain_two,
    w_qkv,
    w_out,
    w_up,
    w_down,
    cotangent,
):
    held_count, patch_count, feature_count = patches.shape
    row_count = cotangent.shape[1]
    lead_count = row_count - patch_count
    task_count = prompt_master.shape[0]
    prompt_table = lax.all_gather(
        prompt_master.astype(jnp.bfloat16), ("dp", "mp"), axis=1, tiled=True
    )
    chosen = tasks == jnp.arange(task_count, dtype=jnp.int32)[None, :]
    lead_part = jnp.dot(
        chosen.astype(jnp.bfloat16), prompt_table, preferred_element_type=jnp.float32
    )
    residual = jnp.concatenate(
        [lead_part.reshape(held_count, lead_count, feature_count), patches.astype(jnp.float32)],
        axis=1,
    )
    row_limit = lengths + lead_count
    w_mix, w_expand, w_reduce, w_rows = (
        lax.all_gather(w_qkv, "dp", axis=0, tiled=True),
        lax.all_gather(w_up, "dp", axis=0, tiled=True),
        lax.all_gather(w_down, "dp", axis=1, tiled=True),
        lax.all_gather(w_out, "dp", axis=1, tiled=True),
    )
    normed = layer_norm(residual, gain_one).astype(jnp.bfloat16)
    mp_rank = lax.axis_index("mp")
    group_normed, group_bound = (
        lax.all_gather(normed, "mp", axis=0, tiled=True),
        lax.all_gather(row_limit.astype(jnp.bfloat16), "mp", axis=0, tiled=True),
    )
    group_limit = group_bound.astype(jnp.int32)
    mixed_qkv, context, logsums = attend_forward(group_normed, group_limit, w_mix, held_count)
    attn_out = lax.psum_scatter(
        rows_term(context, w_rows, "brc,cd->brd"), "mp", scatter_dimension=0, tiled=True
    )
    residual_two = residual + attn_out
    normed_two = layer_norm(residual_two, gain_two).astype(jnp.bfloat16)
    group_two = lax.all_gather(normed_two, "mp", axis=0, tiled=True)
    act_units = expand_units(group_two, w_expand, held_count)
    mlp_out = lax.psum_scatter(
        rows_term(act_units, w_reduce, "brf,fd->brd").astype(jnp.bfloat16),
        "mp",
        scatter_dimension=0,
        tiled=True,
    ).astype(jnp.float32)
    block_sum = residual_two + mlp_out
    live_rows = (jnp.arange(row_count, dtype=jnp.int32)[None, :] < row_limit[:, None]).astype(
        jnp.float32
    )[:, :, None]
    square_sums = jnp.stack(
        [
            jnp.sum(block_sum * block_sum * live_rows),
            jnp.sum(attn_out * attn_out * live_rows),
            jnp.sum(mlp_out * mlp_out * live_rows),
        ]
    )
    live_count = jnp.sum(row_limit).astype(jnp.float32)
    w_mix, w_expand, w_reduce, w_rows = (
        lax.all_gather(w_qkv, "dp", axis=0, tiled=True),
        lax.all_gather(w_up, "dp", axis=0, tiled=True),
        lax.all_gather(w_down, "dp", axis=1, tiled=True),
        lax.all_gather(w_out, "dp", axis=1, tiled=True),
    )
    grad_held = lax.dynamic_slice_in_dim(cotangent, mp_rank * held_count, held_count, 0)
    grad_units = units_back(cotangent, group_two, w_expand, w_reduce, held_count)
    grad_normed_two = lax.psum_scatter(
        rows_term(grad_units, w_expand, "brf,df->brd"), "mp", scatter_dimension=0, tiled=True
    )
    grad_two = grad_held.astype(jnp.float32) + norm_back(residual_two, gain_two, grad_normed_two)
    grad_low = grad_two.astype(jnp.bfloat16)
    grad_context = jnp.einsum(
        "brd,cd->brc",
        lax.all_gather(grad_low, "mp", axis=0, tiled=True),
        w_rows,
        preferred_element_type=jnp.float32,
    ).astype(jnp.bfloat16)
    grad_mixed = attend_back(mixed_qkv, logsums, group_limit, grad_context, held_count)
    grad_normed = lax.psum_scatter(
        rows_term(grad_mixed, w_mix, "brce,dce->brd").astype(jnp.bfloat16),
        "mp",
        scatter_dimension=0,
        tiled=True,
    ).astype(jnp.float32)
    grad_residual = grad_two + norm_back(residual, gain_one, grad_normed)
    patch_grad = grad_residual[:, lead_count:].astype(jnp.bfloat16)
    lead_grad = grad_residual[:, :lead_count].reshape(held_count, lead_count * feature_count)
    task_term = jnp.dot(
        chosen.astype(jnp.float32).T,
        lead_grad,
        precision=lax.Precision.HIGHEST,
        preferred_element_type=jnp.float32,
    )
    task_grad = lax.psum_scatter(task_term, ("dp", "mp"), scatter_dimension=1, tiled=True)
    square = jnp.sum(task_grad * task_grad)
    square, square_sums, live_count = lax.psum((square, square_sums, live_count), ("dp", "mp"))
    grad_norm = jnp.sqrt(square)
    prompt_grad = task_grad * (clip_level / jnp.maximum(grad_norm, clip_level))
    new_first = beta_one * first_moment + (1.0 - beta_one) * prompt_grad
    new_second = beta_two * second_moment + (1.0 - beta_two) * prompt_grad * prompt_grad
    step_size = (
        new_first
        / (1.0 - beta_one**STEP)
        / (jnp.sqrt(new_second / (1.0 - beta_two**STEP)) + adam_eps)
    )
    new_master = prompt_master - learn_rate * (step_size + decay_rate * prompt_master)
    rms_stats = jnp.sqrt(square_sums / (live_count * feature_count))
    return (
        block_sum.astype(jnp.bfloat16),
        patch_grad,
        prompt_grad,
        grad_norm,
        new_first,
        new_second,
        new_master,
        new_master.astype(jnp.bfloat16),
        rms_stats,
    )


def solution(mesh):
    return jax.shard_map(
        body,
        mesh=mesh,
        in_specs=(
            P(("dp", "mp"), None, None),
            P(("dp", "mp")),
            P(("dp", "mp"), None),
            P(None, ("dp", "mp")),
            P(None, ("dp", "mp")),
            P(None, ("dp", "mp")),
            P(),
            P(),
            P("dp", None, "mp"),
            P("mp", "dp"),
            P("dp", "mp"),
            P("mp", "dp"),
            P("dp", None, None),
        ),
        out_specs=(
            P(("dp", "mp"), None, None),
            P(("dp", "mp"), None, None),
            P(None, ("dp", "mp")),
            P(),
            P(None, ("dp", "mp")),
            P(None, ("dp", "mp")),
            P(None, ("dp", "mp")),
            P(None, ("dp", "mp")),
            P(),
        ),
        check_vma=False,
    )
```

profile of v0, /device:TPU:0, one launch (start us, length us, event | category | flops | bytes accessed | tf_op | source)
XLA Modules:
  0.0 797.6 jit_solution(14479353646598021921)
XLA Ops:
  8.8 45.1 %all-gather = bf16[32,1200,8]{1,2,0:T(8,128)(2,1)S(1)} all-gather(bf16[1,1200,8]{1,2,0:T(8,128)(2,1)S(1)} %convert_bitcast_fusion), channel_id=1, replica_groups=mesh['dp'=8,'mp'=4] {'dp','mp'}, dimensions={0}, use_global_device_ids=true | all-gather | bytes 633600 | tf_op jit(solution)/shard_map/all_gather | solution.py:199
  54.1 0.9 reshape.215
  56.4 1.2 multiply_convert_fusion.2
  59.8 6.4 all-reduce
  66.3 33.3 %all_gather.33 = bf16[768,3,192]{2,0,1:T(8,128)(2,1)S(1)} all-gather(bf16[96,3,192]{2,0,1:T(8,128)(2,1)S(1)} %copy-done.9), channel_id=1, replica_groups=mesh['dp'=8,'mp'=4] {'dp'}, dimensions={0}, use_global_device_ids=true | all-gather | bytes 995328 | tf_op jit(solution)/shard_map/all_gather | solution.py:212
  99.6 1.4 copy.60
  101.1 31.4 %all_gather.35 = bf16[192,768]{0,1:T(8,128)(2,1)S(1)} all-gather(bf16[192,96]{0,1:T(8,128)(2,1)S(1)} %copy.61), channel_id=1, replica_groups=mesh['dp'=8,'mp'=4] {'dp'}, dimensions={1}, use_global_device_ids=true | all-gather | bytes 331776 | tf_op jit(solution)/shard_map/all_gather | solution.py:215
  132.5 23.9 %while.44 = (s32[]{:T(128)}, bf16[4,2,256,3,192]{2,4,1,0,3:T(8,128)(2,1)}, bf16[4,2,256,192]{2,3,1,0:T(8,128)(2,1)}, f32[4,2,3,256]{3,2,1,0:T(4,128)S(1)}, s32[4...) while((s32[]{:T(128)}, ...), condition=%wide.region_5.6_spmd, body=%wide.region_2.5_spmd.sunk | while | flops 557185536 | bytes 9401531 | solution.py:86
  133.8 2.1 convolution_convert_fusion.8
  139.8 2.1 convolution_convert_fusion.8
  145.7 2.1 convolution_convert_fusion.8
  151.7 2.1 convolution_convert_fusion.8
  155.6 0.9 copy_dynamic-update-slice_fusion.4
  156.4 4.9 fusion.48
  161.9 55.9 %reduce-scatter.8.cloned.1.call-done = f32[2,256,768]{2,1,0:T(8,128)} async-done(((f32[8,256,768]{2,1,0:T(8,128)}), f32[2,256,768]{2,1,0:T(8,128)}) %reduce-scatter.8.cloned.1.call-update) | async-done | bytes 1572880 | tf_op jit(solution)/shard_map/reduce_scatter | solution.py:225
  217.9 1.7 fusion.61
  220.2 1.1 multiply_convert_fusion.1
  222.2 27.6 %all-gather.9.cloned.1.call-done = bf16[8,256,768]{2,1,0:T(8,128)(2,1)} async-done(((bf16[2,256,768]{2,1,0:T(8,128)(2,1)}), bf16[8,256,768]{2,1,0:T(8,128)(2,1)}) %all-gather.9.cloned.1.call-update) | async-done | bytes 3145744 | tf_op jit(solution)/shard_map/all_gather | solution.py:230
  249.9 1.9 broadcast.219.clone.1
  251.8 30.0 %while.45 = (s32[]{:T(128)}, bf16[4,2,256,768]{3,2,1,0:T(8,128)(2,1)}, s32[4]{0:T(128)S(1)}, bf16[8,256,768]{2,1,0:T(8,128)(2,1)}, bf16[768,768]{1,0:T(8,128)(2,...) while((s32[]{:T(128)}, bf16[4,2,256,768]{3,2,1,0:T(8,128)(2,1)}, s32[4]{0:T(128)S(1)}, ...), condition=%wide.region_10.11_spmd, body=%wide.region_9.10_spmd.sunk | while | flops 629538816 | bytes 2753179 | solution.py:155
  253.0 6.2 fusion.105
  260.5 6.2 fusion.105
  268.0 6.3 fusion.105
  275.5 6.3 fusion.105
  281.8 11.9 %all-gather.13.cloned.1.call-done = bf16[768,768]{0,1:T(8,128)(2,1)} async-done(((bf16[768,96]{0,1:T(8,128)(2,1)}), bf16[768,768]{0,1:T(8,128)(2,1)}) %all-gather.13.cloned.1.call-update) | async-done | bytes 1179664 | tf_op jit(solution)/shard_map/all_gather | solution.py:214
  293.7 6.6 convolution_convert_fusion.3
  300.4 2.4 copy.63
  302.7 1.8 broadcast.219.clone
  304.6 27.5 %while.46 = (s32[]{:T(128)}, bf16[4,2,256,768]{3,2,1,0:T(8,128)(2,1)}, s32[4]{0:T(128)S(1)}, bf16[8,256,768]{2,1,0:T(8,128)(2,1)}, bf16[768,768]{1,0:T(8,128)(2,...) while((s32[]{:T(128)}, ...), condition=%wide.region_13.14_spmd, body=%wide.region_12.13_spmd.sunk | while | flops 1211891712 | bytes 12583627 | solution.py:172
  305.8 2.8 fusion.110
  308.7 3.1 fusion.111
  313.1 2.4 fusion.110
  315.5 3.1 fusion.111
  319.8 2.4 fusion.110
  322.2 3.1 fusion.111
  326.6 2.4 fusion.110
  329.0 3.1 fusion.111
  332.1 7.6 fusion.43
  340.1 57.5 %reduce-scatter.12.cloned.1.call-done = f32[2,256,768]{2,1,0:T(8,128)} async-done(((f32[8,256,768]{2,1,0:T(8,128)}), f32[2,256,768]{2,1,0:T(8,128)}) %reduce-scatter.12.cloned.1.call-update) | async-done | bytes 1572880 | tf_op jit(solution)/shard_map/reduce_scatter | solution.py:258
  397.6 5.1 multiply_reduce_fusion.7
  402.7 2.6 fusion.50
  405.4 28.7 %all-gather.15.cloned.1.call-done = bf16[8,256,768]{2,1,0:T(8,128)(2,1)} async-done(((bf16[2,256,768]{2,1,0:T(8,128)(2,1)}), bf16[8,256,768]{2,1,0:T(8,128)(2,1)}) %all-gather.15.cloned.1.call-update) | async-done | bytes 3145744 | tf_op jit(solution)/shard_map/all_gather | solution.py:265
  434.1 4.0 convolution_convert_fusion.4
  438.1 26.3 %while.47 = (s32[]{:T(128)}, bf16[4,2,256,3,192]{2,4,3,1,0:T(8,128)(2,1)}, s32[4]{0:T(128)S(1)}, bf16[8,256,3,192]{1,3,0,2:T(8,128)(2,1)}, pred[8,256]{1,0:T(8,1...) while((s32[]{:T(128)}, ...), condition=%wide.region_19.20_spmd, body=%wide.region_17.19_spmd.sunk | while | flops 256276992 | bytes 16550583 | solution.py:143
  439.3 1.1 constant_dynamic-slice_fusion.12
  440.4 0.9 constant_dynamic-slice_fusion.11
  445.9 1.1 constant_dynamic-slice_fusion.12
  447.0 0.9 constant_dynamic-slice_fusion.11
  452.4 1.1 constant_dynamic-slice_fusion.12
  453.6 0.9 constant_dynamic-slice_fusion.11
  459.0 1.1 constant_dynamic-slice_fusion.12
  460.1 0.9 constant_dynamic-slice_fusion.11
  464.3 6.4 bitcast_convert_fusion
  471.0 37.8 %reduce-scatter.14.cloned.1.call-done = bf16[2,256,768]{2,1,0:T(8,128)(2,1)} async-done(((bf16[8,256,768]{2,1,0:T(8,128)(2,1)}), bf16[2,256,768]{2,1,0:T(8,128)(2,1)}) %reduce-scatter.14.cloned.1.call-update) | async-done | bytes 786448 | tf_op jit(solution)/shard_map/reduce_scatter | solution.py:270
  508.8 1.9 fusion.41
  510.8 2.3 multiply_add_fusion
  513.1 1.2 copy-done.3
  514.4 18.6 %convolution_bitcast_fusion = f32[38400,8]{1,0:T(8,128)} fusion(f32[2,38400]{1,0:T(2,128)S(1)} %bitcast.212, s32[2]{0:T(128)S(1)} %bitcast.217), kind=kOutput, calls=%fused_computation.76 | convolution fusion | flops 7372816 | bytes 1536008
  533.7 2.0 pad_maximum_fusion.2
  535.7 1.4 slice.51
  537.2 206.9 %reduce-scatter.16.cloned.1.call-done = f32[1200,8]{1,0:T(8,128)} async-done(((f32[38400,8]{1,0:T(8,128)}), f32[1200,8]{1,0:T(8,128)}) %reduce-scatter.16.cloned.1.call-update) | async-done | bytes 38416
  744.0 1.3 copy.79
  745.9 1.3 copy.67
  747.2 39.6 %all-reduce.1 = (f32[]{:T(128)}, f32[3]{0:T(128)S(1)}, f32[]{:T(128)}) all-reduce(f32[]{:T(128)} %multiply_reduce_fusion.8, f32[3]{0:T(128)S(1)} %pad_maximum_fusion.2, f32[]{:T(128)S(6)} %convert_element_type.106), channel_id=1, replica_groups=mesh['dp'=8,'mp'=4] {'dp','mp'}, use_global_device_ids=true, to_apply=%region_25.26 | all-reduce | flops 5 | bytes 40 | tf_op jit(solution)/shard_map/psum | solution.py:287
  (181 shorter events, 41.0 us)
Async XLA Ops:
  8.0 124.5 %all-gather.7.cloned.1.call-start = ((), (), s32[]{:S(2)}) async-start(), calls=%async_computation.5 | async-start | bytes 3932160 | tf_op jit(solution)/shard_map/all_gather | solution.py:220
  8.8 46.1 %copy-start.15 = (s32[2,1]{0,1:T(1,128)S(1)}, s32[2,1]{0,1:T(1,128)}, u32[]{:S(2)}) copy-start(s32[2,1]{0,1:T(1,128)} %param.23) | copy-start | bytes 28
  54.1 1.5 copy-start.7
  55.7 0.7 copy-start.14
  56.4 1.3 copy-start.18
  56.4 2.5 copy-start.17
  56.4 9.8 %copy-start.9 = (bf16[96,3,192]{2,0,1:T(8,128)(2,1)S(1)}, bf16[96,3,192]{2,0,1:T(8,128)(2,1)}, u32[]{:S(2)}) copy-start(bf16[96,3,192]{2,0,1:T(8,128)(2,1)} %param.29) | copy-start | bytes 331780
  57.6 160.2 %reduce-scatter.8.cloned.1.call-start = ((), (), s32[]{:S(2)}) async-start(), calls=%async_computation.6 | async-start | bytes 7864320 | tf_op jit(solution)/shard_map/reduce_scatter | solution.py:225
  66.3 34.7 %copy-start.11 = (bf16[192,96]{1,0:T(8,128)(2,1)S(1)}, bf16[192,96]{1,0:T(8,128)(2,1)}, u32[]{:S(2)}) copy-start(bf16[192,96]{1,0:T(8,128)(2,1)} %param.30) | copy-start | bytes 110596
  99.6 33.0 %copy-start.2 = (bf16[768,3,192]{2,0,1:T(8,128)(2,1)}, bf16[768,3,192]{2,0,1:T(8,128)(2,1)S(1)}, u32[]{:S(2)}) copy-start(bf16[768,3,192]{2,0,1:T(8,128)(2,1)S(1)} %all_gather.33) | copy-start | bytes 2654212
  132.4 24.0 %copy-start.4 = (bf16[192,768]{0,1:T(8,128)(2,1)}, bf16[192,768]{0,1:T(8,128)(2,1)S(1)}, u32[]{:S(2)}) copy-start(bf16[192,768]{0,1:T(8,128)(2,1)S(1)} %all_gather.35) | copy-start | bytes 884740
  161.3 60.9 %all-gather.11.cloned.1.call-start = ((), (), s32[]{:S(2)}) async-start(), calls=%async_computation.8 | async-start | bytes 1327104 | tf_op jit(solution)/shard_map/all_gather | solution.py:213
  161.9 88.0 %all-gather.9.cloned.1.call-start = ((), (), s32[]{:S(2)}) async-start(), calls=%async_computation.7 | async-start | bytes 3932160 | tf_op jit(solution)/shard_map/all_gather | solution.py:230
  219.5 0.7 copy-start.10
  221.4 72.3 %all-gather.13.cloned.1.call-start = ((), (), s32[]{:S(2)}) async-start(), calls=%async_computation.9 | async-start | bytes 1327104 | tf_op jit(solution)/shard_map/all_gather | solution.py:214
  222.0 118.1 %reduce-scatter.10.cloned.1.call-start = ((), (), s32[]{:S(2)}) async-start(), calls=%async_computation.10 | async-start | bytes 3932160 | tf_op jit(solution)/shard_map/reduce_scatter | solution.py:232
  300.3 97.2 %reduce-scatter.12.cloned.1.call-start = ((), (), s32[]{:S(2)}) async-start(), calls=%async_computation.11 | async-start | bytes 7864320 | tf_op jit(solution)/shard_map/reduce_scatter | solution.py:258
  305.8 2.8 copy-start.6
  313.0 2.4 copy-start.6
  319.8 2.4 copy-start.6
  326.6 2.4 copy-start.6
  339.7 94.3 %all-gather.15.cloned.1.call-start = ((), (), s32[]{:S(2)}) async-start(), calls=%async_computation.12 | async-start | bytes 3932160 | tf_op jit(solution)/shard_map/all_gather | solution.py:265
  397.6 5.1 copy-start
  405.3 103.5 %reduce-scatter.14.cloned.1.call-start = ((), (), s32[]{:S(2)}) async-start(), calls=%async_computation.13 | async-start | bytes 3932160 | tf_op jit(solution)/shard_map/reduce_scatter | solution.py:270
  470.7 273.3 %reduce-scatter.16.cloned.1.call-start = ((), (), s32[]{:S(2)}) async-start(), calls=%async_computation.14 | async-start | bytes 20275200
  508.8 1.9 copy-start.1
  508.8 1.9 copy-start.5
  510.8 3.7 copy-start.16
  513.1 1.2 copy-start.3
  535.7 253.0 %copy-start.8 = (f32[8,1200]{1,0:T(8,128)S(1)}, f32[8,1200]{1,0:T(8,128)}, u32[]{:S(2)}) copy-start(f32[8,1200]{1,0:T(8,128)} %param.24) | copy-start | bytes 115204
  535.7 253.0 %copy-start.12 = (f32[8,1200]{1,0:T(8,128)S(1)}, f32[8,1200]{1,0:T(8,128)}, u32[]{:S(2)}) copy-start(f32[8,1200]{1,0:T(8,128)} %param.26) | copy-start | bytes 115204
  535.7 253.0 %copy-start.13 = (f32[8,1200]{1,0:T(8,128)S(1)}, f32[8,1200]{1,0:T(8,128)}, u32[]{:S(2)}) copy-start(f32[8,1200]{1,0:T(8,128)} %param.25) | copy-start | bytes 115204
Sparse Core Ops, SparseCore 0:
  57.8 24.7 all-gather.6
  161.4 56.3 reduce-scatter.7
  405.5 28.5 all-gather.14
  470.8 37.9 reduce-scatter.13
Sparse Core Ops, SparseCore 1:
  164.0 39.5 all-gather.10
  221.5 28.3 all-gather.8
  252.2 41.5 all-gather.12
  300.4 36.3 reduce-scatter.9
  339.8 57.7 reduce-scatter.11
  533.1 210.8 reduce-scatter.15
where the time goes:
time: 799 us; the launch traced here: 798 us
  waiting for transfers between devices  427 us (53%)
  blocking collectives  156 us (20%)
  matrix products  116 us (15%)
  local copies, waits for them, and re-layouts  39.4 us (5%)
  other arithmetic  28 us (4%)
  between operations  19.4 us (2%)
  loops' own time  10.9 us (1%)
    unnamed x11, waiting for transfers between devices  208 us
    reduce_scatter x1, waiting for transfers between devices, body(): lax.psum_scatter(rows_term(grad_units, w_expand, 'brf,df->brd'), 'mp', sc...  57.5 us
    reduce_scatter x1, waiting for transfers between devices, body(): lax.psum_scatter(rows_term(context, w_rows, 'brc,cd->brd'), 'mp', scatter...  55.9 us
    all_gather x1, blocking collectives, body(): lax.all_gather(prompt_master.astype(jnp.bfloat16), ('dp', 'mp'), axis=1,...  45.1 us
    psum x1, blocking collectives, body(): lax.psum((square, square_sums, live_count), ('dp', 'mp'))  39.6 us
    reduce_scatter x1, waiting for transfers between devices, body(): lax.psum_scatter(rows_term(grad_mixed, w_mix, 'brce,dce->brd').astype(jnp...  37.8 us
    all_gather x1, blocking collectives, body(): lax.all_gather(w_qkv, 'dp', axis=0, tiled=True)  33.3 us
    all_gather x1, blocking collectives, body(): lax.all_gather(w_out, 'dp', axis=1, tiled=True)  31.4 us
  transfers between devices with their start and end apart: 10, of which 7 were waited for; matrix products, arithmetic and copies ran while one was open for 9% of the time, Pallas kernels for 0%

commit v1 on v0

--- a/solution.py
+++ b/solution.py
@@ -1,13 +1,18 @@
+import functools
 import math
 
 import jax
 import jax.numpy as jnp
 from jax import lax
+from jax.experimental import pallas as pl
+from jax.experimental.pallas import tpu as pltpu
 from jax.sharding import PartitionSpec as P
 
 HEAD_DIM = 64
 STEP = 10
-
+MESH = pl.DeviceIdType.MESH
+F32 = jnp.float32
+BF16 = jnp.bfloat16
 
 eps_norm = 1e-06
 clip_level = 1.0
@@ -17,6 +22,674 @@
 decay_rate = 0.05
 adam_eps = 1e-08
 
+D = 768
+ROWS = 256
+LEAD = 50
+PATCH = 206
+IMGS = 2
+TASKS = 8
+PART = 1200
+PADP = 1280
+NDEV = 32
+CHUNK = 256
+CHUNKS = 3
+RING = 24
+
+
+def run_if(cond, f):
+    if cond is None:
+        f()
+    else:
+        pl.when(cond())(f)
+
+
+def both(*conds):
+    conds = [c for c in conds if c is not None]
+    if not conds:
+        return None
+
+    def value():
+        out = conds[0]()
+        for c in conds[1:]:
+            out = jnp.logical_and(out, c())
+        return out
+
+    return value
+
+
+class Net:
+    def __init__(self, send_sem, recv_sem):
+        self.send_sem, self.recv_sem = send_sem, recv_sem
+        self.sent = self.used = 0
+        dp, mp = lax.axis_index("dp"), lax.axis_index("mp")
+        z, x, y, c = dp // 2, dp % 2, mp // 2, mp % 2
+        self.z, self.x, self.y, self.c = z, x, y, c
+        self.dp, self.mp = dp, mp
+        self.peer = {
+            "x": (2 * z + 1 - x, mp),
+            "y": (dp, (1 - y) * 2 + c),
+            "c": (dp, 2 * y + 1 - c),
+            "u": (jnp.minimum(2 * z + 2 + x, 6 + x), mp),
+            "d": (jnp.maximum(2 * z - 2 + x, x), mp),
+        }
+        self.ring = [None] * RING
+
+    def alloc(self, n):
+        first = self.used
+        self.used += n
+        return first
+
+    def send(self, way, view, sem, cond=None):
+        i = self.sent % RING
+        self.sent += 1
+        if self.ring[i] is not None:
+            self.wait_sent(i)
+
+        def copy():
+            v = view()
+            return pltpu.make_async_remote_copy(
+                src_ref=v,
+                dst_ref=v,
+                send_sem=self.send_sem.at[i],
+                recv_sem=self.recv_sem.at[sem()],
+                device_id=self.peer[way],
+                device_id_type=MESH,
+            )
+
+        run_if(cond, lambda: copy().start())
+        self.ring[i] = (cond, copy)
+
+    def wait_sent(self, i):
+        cond, copy = self.ring[i]
+        run_if(cond, lambda: copy().wait_send())
+        self.ring[i] = None
+
+    def recv(self, view, sem, cond=None):
+        def wait():
+            v = view()
+            pltpu.make_async_copy(v, v, self.recv_sem.at[sem()]).wait()
+
+        run_if(cond, wait)
+
+    def finish(self):
+        for i in range(RING):
+            if self.ring[i] is not None:
+                self.wait_sent(i)
+
+
+def gather_events(net, G, W, off, split):
+    z, x, y, c = net.z, net.x, net.y, net.c
+    r1, r2, r3, rows = split
+    f_sem, zs_sem, zp_sem, m_sem, l_sem, c_sem = (net.alloc(n) for n in (1, 4, 4, 4, 4, 4))
+    not_top, not_low = (lambda: z < 3), (lambda: z > 0)
+    every = slice(None)
+
+    def V(yy, d, first, last, other=False):
+        def view():
+            core = (1 - c) if other else c
+            cols = pl.ds(pl.multiple_of(core * W, 128), W)
+            return G.at[:, yy, d() if callable(d) else d, pl.ds(first, last - first), cols]
+
+        return view
+
+    def two(p):
+        return lambda: pl.ds(2 * p(), 2)
+
+    def one(p):
+        return lambda: 2 * p() + x
+
+    def at(sem, p):
+        return lambda: sem + p()
+
+    own = lambda: z
+
+    def send(way, yy, d, first, last, sem, cond=None):
+        if last > first:
+            net.send(way, V(yy, d, first, last), sem, cond)
+
+    def planes(k):
+        if k == 0:
+            return [(own, None)]
+        return [(lambda: z - k, lambda: z >= k), (lambda: z + k, lambda: z + k <= 3)]
+
+    def middle(p, cond):
+        send("x", y, one(p), r1, r2, at(m_sem, p), cond)
+        send("y", y, one(p), r2, r3, at(m_sem, p), cond)
+
+    def start():
+        send("x", y, one(own), 0, r1, lambda: f_sem)
+        send("y", y, one(own), r3, rows, lambda: f_sem)
+        send("u", y, one(own), r1, r3, at(zs_sem, own), not_top)
+        send("d", y, one(own), r1, r3, at(zs_sem, own), not_low)
+        middle(own, None)
+
+    def pair(way, p, cond):
+        send(way, y, two(p), 0, r1, at(zp_sem, p), cond)
+        send(way, every, one(p), r3, rows, at(zp_sem, p), cond)
+
+    def first_hop():
+        net.recv(V(y, one(own), 0, r1 + rows - r3), lambda: f_sem)
+        pair("u", own, not_top)
+        pair("d", own, not_low)
+
+    def ways(k):
+        return [(p, cond, w, far) for (p, cond), w, far in zip(planes(k), "ud", (not_top, not_low))]
+
+    def single_hop(k):
+        for p, cond, way, far in ways(k):
+            net.recv(V(y, one(p), r1, r3), at(zs_sem, p), cond)
+            if k < 3:
+                send(way, y, one(p), r1, r3, at(zs_sem, p), both(cond, far))
+            middle(p, cond)
+
+    def pair_hop(k):
+        for p, cond, way, far in ways(k):
+            net.recv(V(y, two(p), 0, r1 + rows - r3), at(zp_sem, p), cond)
+            if k < 3:
+                pair(way, p, both(cond, far))
+
+    def last_hop(k):
+        for p, cond in planes(k):
+            if r3 > r1:
+                net.recv(V(y, one(p), r1, r3), at(m_sem, p), cond)
+            send("y", y, two(p), 0, r2, at(l_sem, p), cond)
+            send("x", every, one(p), r2, rows, at(l_sem, p), cond)
+
+    def to_core(k):
+        for p, cond in planes(k):
+            net.recv(V(y, two(p), 0, rows), at(l_sem, p), cond)
+            send("c", every, two(p), 0, rows, at(c_sem, p), cond)
+
+    def from_core(k):
+        for p, cond in planes(k):
+            net.recv(V(every, two(p), 0, rows, other=True), at(c_sem, p), cond)
+
+    ev = [(off, start), (off + 1, first_hop)]
+    for k in (1, 2, 3):
+        if r3 > r1:
+            ev.append((off + k, functools.partial(single_hop, k)))
+        ev.append((off + 1 + k, functools.partial(pair_hop, k)))
+    for k in (0, 1, 2, 3):
+        ev.append((off + 1 + k + 0.5, functools.partial(last_hop, k)))
+        ev.append((off + 2 + k + 0.3, functools.partial(to_core, k)))
+        ev.append((off + 3 + k + 0.6, functools.partial(from_core, k)))
+    return ev
+
+
+class Events:
+    def __init__(self, items):
+        self.items = sorted(items, key=lambda e: e[0])
+
+    def take(self, limit):
+        out = []
+        while self.items and self.items[0][0] <= limit:
+            out.append(self.items.pop(0)[1])
+        return out
+
+    def run(self, limit):
+        for f in self.take(limit):
+            f()
+
+
+def at_step(t, groups):
+    for j, group in enumerate(groups):
+        if group:
+
+            def go(group=group):
+                for f in group:
+                    f()
+
+            pl.when(t == j)(go)
+
+
+def nn(a, b):
+    return lax.dot_general(a, b, (((1,), (0,)), ((), ())), preferred_element_type=F32)
+
+
+def nt(a, b):
+    return lax.dot_general(a, b, (((1,), (1,)), ((), ())), preferred_element_type=F32)
+
+
+def tn(a, b):
+    return lax.dot_general(a, b, (((0,), (0,)), ((), ())), preferred_element_type=F32)
+
+
+def norm_parts(v):
+    centre = jnp.mean(v, axis=-1, keepdims=True)
+    shifted = v - centre
+    spread = jnp.mean(shifted * shifted, axis=-1, keepdims=True)
+    scaled = lax.rsqrt(spread + eps_norm)
+    return shifted * scaled, scaled
+
+
+def norm_back(v, gain, upstream):
+    normal, scaled = norm_parts(v)
+    weighted = upstream * gain
+    return scaled * (
+        weighted
+        - jnp.mean(weighted, axis=-1, keepdims=True)
+        - normal * jnp.mean(weighted * normal, axis=-1, keepdims=True)
+    )
+
+
+def keep(lanes, low, high):
+    return jnp.where(lanes, low, high)
+
+
+def layer_kernel(
+    patches, lengths, tasks, master, gain_one, gain_two, a_in, u_in, d_in, cot_hbm,
+    out_block, out_patch, out_task, out_stats,
+    GP, GA, GM, LOC, SEL, RES, N1, QKV, PT, CTX, RES2, N2, COT, ACT, GU, MACC, GACC, G2B, DM, LEADR,
+    SEND, RECV, ONEHOT, SREC, STSUM, local_sem, send_sem, recv_sem, all_sem,
+):
+    net = Net(send_sem, recv_sem)
+    z, x, y, c, dp, mp = net.z, net.x, net.y, net.c, net.dp, net.mp
+    device = dp * 4 + mp
+
+    def own_cols(w):
+        return pl.ds(pl.multiple_of(c * w, 128), w)
+
+    cot_copy = pltpu.make_async_copy(cot_hbm.at[pl.ds(mp * IMGS, IMGS)], COT, local_sem.at[0])
+    cot_copy.start()
+    copies = [pltpu.make_async_copy(a_in, GA.at[0, y, dp, :, own_cols(D)], local_sem.at[1])]
+    for i in range(CHUNKS):
+        for j, w in enumerate((u_in, d_in)):
+            copies.append(
+                pltpu.make_async_copy(
+                    w.at[:, pl.ds(CHUNK * i, CHUNK)],
+                    GM.at[i, j, y, dp, :, own_cols(CHUNK)],
+                    local_sem.at[2 + 2 * i + j],
+                )
+            )
+    for copy in copies:
+        copy.start()
+    barrier = pltpu.get_barrier_semaphore()
+    for i in range(8):
+        for j in range(4):
+            @pl.when(jnp.logical_or(dp != i, mp != j))
+            def _():
+                pl.semaphore_signal(barrier, inc=1, device_id=(i, j), device_id_type=MESH)
+
+    LOC[:, 0:PART] = master[...]
+    lane = lax.broadcasted_iota(jnp.int32, (TASKS, PADP - PART), 1)
+    LOC[:, PART:PADP] = jnp.where(
+        lane == 0, tasks[0, 0].astype(F32), jnp.where(lane == 1, tasks[1, 0].astype(F32), 0.0)
+    )
+    half = PADP // 2
+    GP[0, pl.ds(y, 1), pl.ds(dp, 1), :, own_cols(half)] = (
+        jnp.concatenate([LOC[:, 0:half], LOC[:, half:PADP]], axis=0).astype(BF16)[None, None]
+    )
+    for copy in copies:
+        copy.wait()
+    pl.semaphore_wait(barrier, NDEV - 1)
+
+    split = (32, 48, 64, 96)
+    ev = gather_events(net, GP, half, -0.5, (16, 16, 16, 16))
+    ev += gather_events(net, GA, D, 0.0, split)
+    for i in range(CHUNKS):
+        ev += gather_events(net, GM.at[i], CHUNK, 1.51 * (i + 1), split)
+    ev = [(-1 + 0.01 * k if f.__name__ == "start" else k, f) if hasattr(f, "__name__") else (k, f) for k, f in ev]
+    events = Events(ev)
+
+    g1 = gain_one[...]
+    g2 = gain_two[...]
+    limits = [lengths[b] + LEAD for b in range(IMGS)]
+    live = [
+        (lax.broadcasted_iota(jnp.int32, (ROWS, 1), 0) < limits[b]).astype(F32) for b in range(IMGS)
+    ]
+
+    events.run(0.5)
+    for b in range(IMGS):
+        RES[b, LEAD:ROWS, :] = patches[b].astype(F32)
+    MACC[...] = jnp.zeros_like(MACC)
+    GACC[...] = jnp.zeros_like(GACC)
+    SEND[...] = jnp.zeros_like(SEND)
+    events.run(6.11)
+
+    task_rows = lax.broadcasted_iota(jnp.int32, (TASKS, 1), 0)
+
+    def pick(d, _):
+        dd, mm = d // 4, d % 4
+        raw = GP[0, mm // 2, dd, :, pl.ds(pl.multiple_of((mm % 2) * half, 128), half)].astype(F32)
+        low, high = raw[0:8], raw[8:16]
+        rep, j = d // 16, d % 16
+        for b in range(IMGS):
+            hot = (task_rows == tasks[b, 0]).astype(F32)
+            row = 2 * rep + b
+            SEL[j, pl.ds(row, 1), 0:half] = jnp.sum(low * hot, axis=0, keepdims=True)
+            SEL[j, pl.ds(row, 1), half:PADP] = jnp.sum(high * hot, axis=0, keepdims=True)
+        base = PART - half
+        for b in range(IMGS):
+            which = high[0:1, base + b : base + b + 1]
+            ONEHOT[d, b] = (
+                lax.broadcasted_iota(jnp.int32, (TASKS, 128), 0).astype(F32) == which
+            ).astype(F32)
+        return 0
+
+    lax.fori_loop(0, NDEV, pick, 0)
+    wide = lax.broadcasted_iota(jnp.int32, (4, D), 1)
+    for r in range(25):
+        j, off = (D * r) // PART, (D * r) % PART
+        first = min(D, PART - off)
+        low = SEL[j, 0:4, :]
+        seg = (pltpu.roll(low, PADP - off, 1) if off else low)[:, 0:D]
+        if first < D:
+            seg = jnp.where(wide < first, seg, pltpu.roll(SEL[j + 1, 0:4, :], first, 1)[:, 0:D])
+        for rep in range(2):
+            for b in range(IMGS):
+                RES[b, 25 * rep + r : 25 * rep + r + 1, :] = seg[2 * rep + b : 2 * rep + b + 1]
+
+    for b in range(IMGS):
+        N1[b] = (norm_parts(RES[b])[0] * g1).astype(BF16)
+    events.run(6.61)
+
+    def weight(ref, core, first, width, span):
+        cols = pl.ds(pl.multiple_of(core * span + first, 128), width)
+        return ref[:, :, cols].reshape(D, width)
+
+    left = lax.broadcasted_iota(jnp.int32, (ROWS, 128), 1) < HEAD_DIM
+    scale = 1.0 / math.sqrt(HEAD_DIM)
+    wide = lax.broadcasted_iota(jnp.int32, (1, 640), 1)
+    q_scale = jnp.where((wide < 128) | ((wide >= 384) & (wide < 448)), scale, 1.0)
+
+    def split_keys(first, step, n):
+        return [events.take(first + step * (j + 1)) for j in range(n)]
+
+    groups = split_keys(6.61, 0.15, 4)
+
+    def project(t, _):
+        at_step(t, groups)
+        w = weight(GA.at[0, t // 2], t % 2, 0, 640, D)
+        mixed = nn(N1[...].reshape(IMGS * ROWS, D), w).astype(BF16).astype(F32) * q_scale
+        QKV[t] = mixed.astype(BF16).reshape(IMGS, ROWS, 640)
+        return 0
+
+    lax.fori_loop(0, 4, project, 0)
+
+    key_rows = lax.broadcasted_iota(jnp.int32, (ROWS, ROWS), 0)
+    zero = jnp.zeros((), BF16)
+    groups_a = split_keys(7.2, 0.15, 8)
+
+    def attend(t, _):
+        at_step(t, groups_a)
+        b, m = t // 4, t % 4
+        tile = lambda i: QKV[m, b, :, 128 * i : 128 * i + 128]
+        q01, k01, v01, q2v2, k2 = (tile(i) for i in range(5))
+        mask = key_rows < (lengths[b] + LEAD)
+
+        def soft(keys, queries):
+            s = jnp.where(mask, nt(keys, queries), -1e30)
+            e = jnp.exp(s - jnp.max(s, axis=0, keepdims=True))
+            return (e * (1.0 / jnp.sum(e, axis=0, keepdims=True))).astype(BF16)
+
+        p0 = soft(k01, keep(left, q01, zero))
+        p1 = soft(k01, keep(left, zero, q01))
+        p2 = soft(k2, keep(left, q2v2, zero))
+        PT[t, 0], PT[t, 1], PT[t, 2] = p0, p1, p2
+        CTX[b, :, pl.ds(pl.multiple_of(m * 256, 128), 128)] = keep(left, 0.0, tn(p2, q2v2)).astype(BF16)
+        CTX[b, :, pl.ds(pl.multiple_of(m * 256 + 128, 128), 128)] = keep(
+            left, tn(p0, v01), tn(p1, v01)
+        ).astype(BF16)
+        return 0
+
+    lax.fori_loop(0, 8, attend, 0)
+
+    sums = [jnp.zeros((1, 1), F32) for _ in range(3)]
+
+    def total(v):
+        return jnp.sum(jnp.sum(v, axis=0, keepdims=True), axis=1, keepdims=True)
+
+    for b in range(IMGS):
+        events.run(8.4 + 0.2 * (b + 1))
+        attn = jnp.zeros((ROWS, D), F32)
+        for m in range(4):
+            attn += nt(CTX[b, :, 256 * m : 256 * m + 256], weight(GA.at[0, m // 2], m % 2, 512, 256, D))
+        sums[1] += total(attn * attn * live[b])
+        res2 = RES[b] + attn
+        RES2[b] = res2
+        N2[b] = (norm_parts(res2)[0] * g2).astype(BF16)
+    cot_copy.wait()
+
+    done = [1.51 * (i + 1) + 6.61 for i in range(CHUNKS)]
+    groups_m = [[], [], [], [], [], []]
+    for i in range(CHUNKS):
+        groups_m[2 * i] = events.take(done[i])
+        groups_m[2 * i + 1] = events.take(done[i] + 0.6)
+
+    def feed(t, _):
+        at_step(t, groups_m)
+        i, yy = t // 2, t % 2
+        rows2 = N2[...].reshape(IMGS * ROWS, D)
+        cot = COT[...].reshape(IMGS * ROWS, D)
+        for core in range(2):
+            up = nn(rows2, weight(GM.at[i, 0, yy], core, 0, CHUNK, CHUNK))
+            back = nn(cot, weight(GM.at[i, 1, yy], core, 0, CHUNK, CHUNK))
+            cumul = 0.5 * (1.0 + lax.erf(up * 0.7071067811865476))
+            density = jnp.exp(-0.5 * up * up) * 0.3989422804014327
+            ACT[:, CHUNK * core : CHUNK * (core + 1)] = (up * cumul).astype(BF16)
+            GU[:, CHUNK * core : CHUNK * (core + 1)] = (back * (cumul + up * density)).astype(BF16)
+        wide_d = weight(GM.at[i, 1, yy], 0, 0, 2 * CHUNK, CHUNK)
+        MACC[...] += nt(ACT[...], wide_d).reshape(IMGS, ROWS, D)
+        wide_u = weight(GM.at[i, 0, yy], 0, 0, 2 * CHUNK, CHUNK)
+        GACC[...] += nt(GU[...], wide_u).reshape(IMGS, ROWS, D)
+        return 0
+
+    lax.fori_loop(0, 2 * CHUNKS, feed, 0)
+    events.run(1e9)
+
+    for b in range(IMGS):
+        mlp = MACC[b]
+        block = RES2[b] + mlp
+        out_block[b] = block.astype(BF16)
+        sums[0] += total(block * block * live[b])
+        sums[2] += total(mlp * mlp * live[b])
+        g = COT[b].astype(F32) + norm_back(RES2[b], g2, GACC[b])
+        MACC[b] = g
+        G2B[b] = g.astype(BF16)
+
+    def attend_back(t, _):
+        b, m = t // 4, t % 4
+        tile = lambda i: QKV[m, b, :, 128 * i : 128 * i + 128]
+        q01, k01, v01, q2v2, k2 = (tile(i) for i in range(5))
+        cols = pl.ds(pl.multiple_of((m % 2) * D + 512, 128), 256)
+        w = GA[0, m // 2, :, :, cols].reshape(D, 256)
+        dctx = nn(G2B[b], w).astype(BF16)
+        c2, c01 = dctx[:, 0:128], dctx[:, 128:256]
+
+        def back(p, v, grad):
+            pf = p.astype(F32)
+            dp_ = nt(v, grad)
+            inner = jnp.sum(pf * dp_, axis=0, keepdims=True)
+            return (pf * (dp_ - inner)).astype(BF16)
+
+        p0, p1, p2 = PT[t, 0], PT[t, 1], PT[t, 2]
+        s0 = back(p0, keep(left, v01, zero), c01)
+        s1 = back(p1, keep(left, zero, v01), c01)
+        s2 = back(p2, keep(left, zero, q2v2), c2)
+        DM[m, b, :, 0:128] = (keep(left, tn(s0, k01), tn(s1, k01)) * scale).astype(BF16)
+        DM[m, b, :, 128:256] = keep(left, nn(s0, q01), nn(s1, q01)).astype(BF16)
+        DM[m, b, :, 256:384] = keep(left, nn(p0, c01), nn(p1, c01)).astype(BF16)
+        DM[m, b, :, 384:512] = keep(left, tn(s2, k2) * scale, nn(p2, c2)).astype(BF16)
+        DM[m, b, :, 512:640] = keep(left, nn(s2, q2v2), 0.0).astype(BF16)
+        return 0
+
+    lax.fori_loop(0, 8, attend_back, 0)
+
+    for b in range(IMGS):
+        grad = jnp.zeros((ROWS, D), F32)
+        for m in range(4):
+            grad += nt(DM[m, b], weight(GA.at[0, m // 2], m % 2, 0, 640, D))
+        grad = MACC[b] + norm_back(RES[b], g1, grad)
+        GACC[b] = grad
+        out_patch[b] = GACC[b, LEAD:ROWS, :].astype(BF16)
+
+    for rep in range(2):
+        for b in range(IMGS):
+            LEADR[:, 2 * rep + b : 2 * rep + b + 1, :] = GACC[b, 25 * rep : 25 * rep + 25, :][:, None, :]
+    wide = lax.broadcasted_iota(jnp.int32, (4, PADP), 1)
+    for q in range(16):
+        r, off = (PART * q) // D, (PART * q) % D
+        msg, have = None, -off
+        while have < PART:
+            row = jnp.concatenate([LEADR[r, 0:4, :], jnp.zeros((4, PADP - D), F32)], axis=1)
+            moved = pltpu.roll(row, have % PADP, 1) if have % PADP else row
+            msg = moved if msg is None else jnp.where(wide < have, msg, moved)
+            have += D
+            r += 1
+        msg = jnp.where(wide < PART, msg, 0.0)
+        SEND[q] = msg[0:2]
+        SEND[16 + q] = msg[2:4]
+
+    def swap(d, what, start):
+        i, j = d // 4, d % 4
+
+        @pl.when(d != device)
+        def _():
+            pltpu.make_async_remote_copy(
+                src_ref=what(d, True),
+                dst_ref=what(device, False),
+                send_sem=all_sem.at[2 * start],
+                recv_sem=all_sem.at[2 * start + 1],
+                device_id=(i, j),
+                device_id_type=MESH,
+            ).start()
+
+    def to_owner(d, _):
+        swap(d, lambda k, mine: SEND.at[k] if mine else RECV.at[k], 0)
+        return 0
+
+    lax.fori_loop(0, NDEV, to_owner, 0)
+    RECV[pl.ds(device, 1)] = SEND[pl.ds(device, 1)]
+    others = RECV.at[pl.ds(0, NDEV - 1)]
+    pltpu.make_async_copy(others, others, all_sem.at[1]).wait()
+
+    def add(s, acc):
+        acc = acc + jnp.concatenate([ONEHOT[s, 0]] * (PADP // 128), axis=1) * RECV[s, 0:1, :]
+        return acc + jnp.concatenate([ONEHOT[s, 1]] * (PADP // 128), axis=1) * RECV[s, 1:2, :]
+
+    task_grad = lax.fori_loop(0, NDEV, add, jnp.zeros((TASKS, PADP), F32))
+    square = total(task_grad * task_grad)
+    lane = lax.broadcasted_iota(jnp.int32, (8, 128), 1)
+    count = (limits[0] + limits[1]).astype(F32)
+    stats = jnp.where(lane == 0, square, jnp.where(lane == 1, sums[0], jnp.where(lane == 2, sums[1], jnp.where(
+        lane == 3, sums[2], jnp.where(lane == 4, count, 0.0)))))
+    STSUM[...] = stats
+    SREC[pl.ds(device, 1)] = stats[None]
+
+    def to_all(d, _):
+        swap(d, lambda k, mine: STSUM if mine else SREC.at[k], 1)
+        return 0
+
+    lax.fori_loop(0, NDEV, to_all, 0)
+    out_task[...] = task_grad[:, 0:PART]
+    others2 = SREC.at[pl.ds(0, NDEV - 1)]
+    pltpu.make_async_copy(others2, others2, all_sem.at[3]).wait()
+    out_stats[...] = jnp.sum(SREC[...], axis=0)
+    pltpu.make_async_copy(others, others, all_sem.at[0]).wait()
+    pltpu.make_async_copy(others2, others2, all_sem.at[2]).wait()
+    net.finish()
+
+
+def update_kernel(
+    task_grad, stats, master, first_moment, second_moment, block_in, patch_in,
+    out_grad, out_first, out_second, out_master, out_copy, out_small, block_out, patch_out,
+):
+    block_out[...] = block_in[...]
+    patch_out[...] = patch_in[...]
+    st = stats[0:1, :]
+    square = st[0:1, 0:1]
+    norm = jnp.sqrt(square)
+    grad = task_grad[...] * (clip_level / jnp.maximum(norm, clip_level))
+    first = beta_one * first_moment[...] + (1.0 - beta_one) * grad
+    second = beta_two * second_moment[...] + (1.0 - beta_two) * grad * grad
+    step_size = (
+        first / (1.0 - beta_one**STEP) / (jnp.sqrt(second / (1.0 - beta_two**STEP)) + adam_eps)
+    )
+    old = master[...]
+    new = old - learn_rate * (step_size + decay_rate * old)
+    out_grad[...] = grad
+    out_first[...] = first
+    out_second[...] = second
+    out_master[...] = new
+    out_copy[...] = new.astype(BF16)
+    lane = lax.broadcasted_iota(jnp.int32, (1, 128), 1)
+    inside = jnp.where(lane == 0, square, st / (st[0:1, 4:5] * D))
+    out_small[...] = jnp.sqrt(inside)
+
+
+def fast_body(
+    patches, lengths, tasks, prompt_master, first_moment, second_moment,
+    gain_one, gain_two, w_qkv, w_out, w_up, w_down, cotangent,
+):
+    heads = w_qkv.reshape(96, 3, 3, HEAD_DIM)
+    outs = w_out.T.reshape(96, 3, HEAD_DIM)
+    order = [heads[:, 0, 0], heads[:, 0, 1], heads[:, 1, 0], heads[:, 1, 1], heads[:, 2, 0], heads[:, 2, 1],
+             heads[:, 0, 2], heads[:, 2, 2], heads[:, 1, 2], outs[:, 2], outs[:, 0], outs[:, 1]]
+    a_in = jnp.concatenate(order, axis=1)
+    d_in = w_down.T
+    vmem = pl.BlockSpec(memory_space=pltpu.VMEM)
+    smem = pl.BlockSpec(memory_space=pltpu.SMEM)
+    anywhere = pl.BlockSpec(memory_space=pl.ANY)
+    V = pltpu.VMEM
+    block, patch, task, stats = pl.pallas_call(
+        layer_kernel,
+        out_shape=[
+            jax.ShapeDtypeStruct((IMGS, ROWS, D), BF16),
+            jax.ShapeDtypeStruct((IMGS, PATCH, D), BF16),
+            jax.ShapeDtypeStruct((TASKS, PART), F32),
+            jax.ShapeDtypeStruct((8, 128), F32),
+        ],
+        in_specs=[vmem, smem, smem, vmem, vmem, vmem, vmem, vmem, vmem, anywhere],
+        out_specs=[vmem] * 4,
+        scratch_shapes=[
+            V((1, 2, 8, 16, PADP), BF16),
+            V((1, 2, 8, 96, 2 * D), BF16),
+            V((CHUNKS, 2, 2, 8, 96, 2 * CHUNK), BF16),
+            V((TASKS, PADP), F32),
+            V((16, 4, PADP), F32),
+            V((IMGS, ROWS, D), F32),
+            V((IMGS, ROWS, D), BF16),
+            V((4, IMGS, ROWS, 640), BF16),
+            V((8, 3, ROWS, ROWS), BF16),
+            V((IMGS, ROWS, 1024), BF16),
+            V((IMGS, ROWS, D), F32),
+            V((IMGS, ROWS, D), BF16),
+            V((IMGS, ROWS, D), BF16),
+            V((IMGS * ROWS, 2 * CHUNK), BF16),
+            V((IMGS * ROWS, 2 * CHUNK), BF16),
+            V((IMGS, ROWS, D), F32),
+            V((IMGS, ROWS, D), F32),
+            V((IMGS, ROWS, D), BF16),
+            V((4, IMGS, ROWS, 640), BF16),
+            V((25, 4, D), F32),
+            V((NDEV, IMGS, PADP), F32),
+            V((NDEV, IMGS, PADP), F32),
+            V((NDEV, IMGS, TASKS, 128), F32),
+            V((NDEV, 8, 128), F32),
+            V((8, 128), F32),
+            pltpu.SemaphoreType.DMA((8,)),
+            pltpu.SemaphoreType.DMA((RING,)),
+            pltpu.SemaphoreType.DMA((21 * (2 + CHUNKS),)),
+            pltpu.SemaphoreType.DMA((4,)),
+        ],
+        compiler_params=pltpu.CompilerParams(
+            collective_id=0, has_side_effects=True, vmem_limit_bytes=58 << 20
+        ),
+    )(patches, lengths, tasks, prompt_master, gain_one[None, :], gain_two[None, :], a_in, w_up, d_in, cotangent)
+    grad, first, second, master, copy, small, block_out, patch_out = pl.pallas_call(
+        update_kernel,
+        out_shape=[jax.ShapeDtypeStruct((TASKS, PART), F32)] * 4
+        + [
+            jax.ShapeDtypeStruct((TASKS, PART), BF16),
+            jax.ShapeDtypeStruct((1, 128), F32),
+            jax.ShapeDtypeStruct((IMGS, ROWS, D), BF16),
+            jax.ShapeDtypeStruct((IMGS, PATCH, D), BF16),
+        ],
+        in_specs=[vmem] * 7,
+        out_specs=[vmem] * 8,
+    )(task, stats, prompt_master, first_moment, second_moment, block, patch)
+    return block_out, patch_out, grad, small[0, 0], first, second, master, copy, small[0, 1:4]
+
 
 def layer_norm(values, gain):
     centre = jnp.mean(values, axis=-1, keepdims=True)
@@ -25,7 +698,7 @@
     return shifted * lax.rsqrt(spread + eps_norm) * gain
 
 
-def norm_back(values, gain, upstream):
+def whole_norm_back(values, gain, upstream):
     centre = jnp.mean(values, axis=-1, keepdims=True)
     shifted = values - centre
     spread = jnp.mean(shifted * shifted, axis=-1, keepdims=True)
@@ -258,7 +931,7 @@
     grad_normed_two = lax.psum_scatter(
         rows_term(grad_units, w_expand, "brf,df->brd"), "mp", scatter_dimension=0, tiled=True
     )
-    grad_two = grad_held.astype(jnp.float32) + norm_back(residual_two, gain_two, grad_normed_two)
+    grad_two = grad_held.astype(jnp.float32) + whole_norm_back(residual_two, gain_two, grad_normed_two)
     grad_low = grad_two.astype(jnp.bfloat16)
     grad_context = jnp.einsum(
         "brd,cd->brc",
@@ -273,7 +946,7 @@
         scatter_dimension=0,
         tiled=True,
     ).astype(jnp.float32)
-    grad_residual = grad_two + norm_back(residual, gain_one, grad_normed)
+    grad_residual = grad_two + whole_norm_back(residual, gain_one, grad_normed)
     patch_grad = grad_residual[:, lead_count:].astype(jnp.bfloat16)
     lead_grad = grad_residual[:, :lead_count].reshape(held_count, lead_count * feature_count)
     task_term = jnp.dot(
@@ -310,8 +983,9 @@
 
 
 def solution(mesh):
+    small = mesh.shape["dp"] == 8 and mesh.shape["mp"] == 4
     return jax.shard_map(
-        body,
+        fast_body if small else body,
         mesh=mesh,
         in_specs=(
             P(("dp", "mp"), None, None),

time: 799 us -> 127 us (0.16)
  waiting for transfers between devices: 427 us -> 0 us
  blocking collectives: 156 us -> 0 us
  matrix products: 116 us -> 0 us
  Pallas kernels: 0 us -> 112 us
  other arithmetic: 28 us -> 0 us
  local copies, waits for them, and re-layouts: 39.4 us -> 13.4 us
  between operations: 19.4 us -> 0.72 us
  loops' own time: 10.9 us -> 0 us
    unnamed x11 -> x0, waiting for transfers between devices: 208 us -> none
    reduce_scatter x4 -> x0, waiting for transfers between devices: 151 us -> none  [the longest x1 57.5 us: body(): lax.psum_scatter(rows_term(grad_units, w_expand, 'brf,df->brd'), 'mp', sc...]
    pallas_call x0 -> x2, Pallas kernels: none -> 112 us  [the longest x1 109 us: fast_body(): pl.pallas_call(layer_kernel, out_shape=[jax.ShapeDtypeStruct((IMGS, ROWS,...]
    all_gather x3 -> x0, blocking collectives: 110 us -> none  [the longest x1 45.1 us: body(): lax.all_gather(prompt_master.astype(jnp.bfloat16), ('dp', 'mp'), axis=1,...]
    dot_general x50 -> x0, matrix products: 97 us -> none  [the longest x4 25.4 us: rows_term(): return jnp.einsum(form, source, weight, preferred_element_type=jnp.float32)]
    all_gather x5 -> x0, waiting for transfers between devices: 68.2 us -> none  [the longest x1 28.7 us: body(): lax.all_gather(grad_low, 'mp', axis=0, tiled=True)]
    psum x1 -> x0, blocking collectives: 39.6 us -> none  [body(): lax.psum((square, square_sums, live_count), ('dp', 'mp'))]
    unnamed x1 -> x0, matrix products: 18.6 us -> none
  transfers between devices with their start and end apart: 10 -> 0, of which waited for: 7 -> 0; matrix products, arithmetic and copies ran while one was open for 9% -> 0% of each run, Pallas kernels for 0% -> 0%
where the time goes in v1:
time: 127 us; the launch traced here: 126 us
  Pallas kernels  112 us (88%)
  local copies, waits for them, and re-layouts  13.4 us (11%)
    pallas_call x1, Pallas kernels, fast_body(): pl.pallas_call(layer_kernel, out_shape=[jax.ShapeDtypeStruct((IMGS, ROWS,...  109 us
    unnamed x16, local copies, waits for them, and re-layouts  8.04 us
    pallas_call x1, Pallas kernels, fast_body(): pl.pallas_call(update_kernel, out_shape=[jax.ShapeDtypeStruct((TASKS, PAR...  2.64 us

profile of v1, /device:TPU:0, one launch (start us, length us, event | category | flops | bytes accessed | tf_op | source)
XLA Modules:
  0.0 126.2 jit_solution(1977793814804071563)
XLA Ops:
  0.6 1.3 %copy.39.tasks = s32[2,1]{1,0:T(2,128)} copy(s32[2,1]{0,1:T(1,128)} %param.15) | data formatting | bytes 16 | tf_op args[2]
  1.9 1.3 %broadcast_in_dim.6.gain_one = f32[1,768]{1,0:T(1,128)} reshape(f32[768]{0:T(1024)} %param.19) | data formatting | bytes 6144 | tf_op jit(solution)/shard_map/broadcast_in_dim | solution.py:678
  3.2 1.3 %broadcast_in_dim.7.gain_two = f32[1,768]{1,0:T(1,128)} reshape(f32[768]{0:T(1024)} %param.20) | data formatting | bytes 6144 | tf_op jit(solution)/shard_map/broadcast_in_dim | solution.py:678
  4.5 0.8 fusion.1
  5.2 0.1 copy.52
  5.3 0.1 copy.51
  5.4 0.1 copy.50
  5.6 1.1 copy.25
  6.7 0.1 copy.49
  6.8 0.1 copy.48
  6.9 0.1 copy.47
  7.0 0.1 copy.46
  7.1 0.1 copy.45
  7.2 0.1 copy.44
  7.3 0.1 copy.43
  7.5 0.1 copy.42
  7.6 0.1 copy.41
  7.7 0.8 concatenate.3.a_in
  8.5 2.0 %copy.38.patches = bf16[2,206,768]{2,1,0:T(8,128)(2,1)} copy(bf16[2,206,768]{2,0,1:T(2,128)(2,1)} %param.13) | data formatting | bytes 1265664 | tf_op args[0]
  10.5 109.5 %shard_map.196 = (bf16[2,256,768]{2,1,0:T(8,128)(2,1)}, bf16[2,206,768]{2,1,0:T(8,128)(2,1)}, f32[8,1200]{1,0:T(8,128)}, f32[8,128]{1,0:T(8,128)}) custom-call(bf16[2,206,768]{2,1,0:T(8,128)(2,1)} %copy.38.patches, s32[2]{0:T(128)} %lengths.1, s32[2,1]{1,0:T(2,128)} %copy.39.tasks, f32[8,1200]{1,0:T(8,128)} %master.3, f32[1,768]{1,0:T(1,128)} %broadcast_in_dim.6.gain_one, ...), custom_call_target="tpu_custom_call" | custom-call | tf_op jit(solution)/shard_map/pallas_call | solution.py:634
  120.0 2.6 %shard_map.197 = (f32[8,1200]{1,0:T(8,128)}, f32[8,1200]{1,0:T(8,128)}, f32[8,1200]{1,0:T(8,128)}, f32[8,1200]{1,0:T(8,128)}, bf16[8,1200]{1,0:T(8,128)(2,1)}, /...) custom-call(f32[8,1200]{1,0:T(8,128)} %get-tuple-element.21.task_grad, ...), custom_call_target="tpu_custom_call" | custom-call | tf_op jit(solution)/shard_map/pallas_call | solution.py:679
  122.6 1.2 slice_bitcast_fusion
  123.8 2.4 %copy.40 = bf16[2,206,768]{2,0,1:T(2,128)(2,1)} copy(bf16[2,206,768]{2,1,0:T(8,128)(2,1)} %get-tuple-element.43) | data formatting | bytes 1265664
  (1 shorter events, 0.0 us)

commit v2 on v1

--- a/solution.py
+++ b/solution.py
@@ -31,9 +31,29 @@
 PART = 1200
 PADP = 1280
 NDEV = 32
-CHUNK = 256
-CHUNKS = 3
+CHUNKS = (256, 256, 256)
+ORDER = (
+    (0, 28, 112, 84, 56, 4, 32, 37, 44,),
+    (13, 17, 16, 60, 72, 14, 18, 48, 41, 38, 65, 20, 45, 22, 15, 21, 93, 19, 42, 46, 52, 39, 23, 69, 26, 25, 66, 73, 27, 24,),
+    (49, 88,),
+    (43, 47, 67, 94, 70, 121, 53, 50, 100, 74, 51, 95, 54, 97, 101, 116, 55,),
+    (71, 128, 76, 75,),
+    (77, 98, 122, 104,),
+    (102,),
+    (125, 129, 105, 108,),
+    (78, 80, 79, 132,),
+    (123,),
+    (81, 99, 103, 83,),
+    (126, 130, 109, 82, 136, 106,),
+    (127, 131, 107,),
+    (110, 133, 111, 134,),
+    (137, 135,),
+    (138, 139,),
+    (),
+    (),
+)
 RING = 24
+ATT = 4
 
 
 def run_if(cond, f):
@@ -117,10 +137,11 @@
                 self.wait_sent(i)
 
 
-def gather_events(net, G, W, off, split):
+def gather_events(net, G, W, split):
     z, x, y, c = net.z, net.x, net.y, net.c
     r1, r2, r3, rows = split
-    f_sem, zs_sem, zp_sem, m_sem, l_sem, c_sem = (net.alloc(n) for n in (1, 4, 4, 4, 4, 4))
+    some = 4 if r3 > r1 else 0
+    f_sem, zs_sem, zp_sem, m_sem, l_sem, c_sem = (net.alloc(n) for n in (1, some, 4, some, 4, 4))
     not_top, not_low = (lambda: z < 3), (lambda: z > 0)
     every = slice(None)
 
@@ -204,31 +225,8 @@
         for p, cond in planes(k):
             net.recv(V(every, two(p), 0, rows, other=True), at(c_sem, p), cond)
 
-    ev = [(off, start), (off + 1, first_hop)]
-    for k in (1, 2, 3):
-        if r3 > r1:
-            ev.append((off + k, functools.partial(single_hop, k)))
-        ev.append((off + 1 + k, functools.partial(pair_hop, k)))
-    for k in (0, 1, 2, 3):
-        ev.append((off + 1 + k + 0.5, functools.partial(last_hop, k)))
-        ev.append((off + 2 + k + 0.3, functools.partial(to_core, k)))
-        ev.append((off + 3 + k + 0.6, functools.partial(from_core, k)))
-    return ev
-
-
-class Events:
-    def __init__(self, items):
-        self.items = sorted(items, key=lambda e: e[0])
-
-    def take(self, limit):
-        out = []
-        while self.items and self.items[0][0] <= limit:
-            out.append(self.items.pop(0)[1])
-        return out
-
-    def run(self, limit):
-        for f in self.take(limit):
-            f()
+    kinds = (start, first_hop, single_hop, pair_hop, last_hop, to_core, from_core)
+    return [f if i < 2 else functools.partial(f, k) for i, f in enumerate(kinds) for k in range(4)]
 
 
 def at_step(t, groups):
@@ -277,43 +275,67 @@
 
 
 def layer_kernel(
-    patches, lengths, tasks, master, gain_one, gain_two, a_in, u_in, d_in, cot_hbm,
+    patches, lengths, tasks, master, gain_one, gain_two, qkv_in, out_in, u_in, d_in, cot_hbm,
     out_block, out_patch, out_task, out_stats,
-    GP, GA, GM, LOC, SEL, RES, N1, QKV, PT, CTX, RES2, N2, COT, ACT, GU, MACC, GACC, G2B, DM, LEADR,
-    SEND, RECV, ONEHOT, SREC, STSUM, local_sem, send_sem, recv_sem, all_sem,
+    GP, GA, GM0, GM1, GM2, LOC, SEL, RES, N1, QKV, PT, CTX, RES2, N2, COT, ACT, GU, MACC, GACC, G2, G2B, DM, DC, LEADR,
+    PAIR, PIN, BOUT, SEND, RECV, ONEHOT, SREC, STSUM, local_sem, send_sem, recv_sem, all_sem,
 ):
     net = Net(send_sem, recv_sem)
     z, x, y, c, dp, mp = net.z, net.x, net.y, net.c, net.dp, net.mp
     device = dp * 4 + mp
+    GMS = (GM0, GM1, GM2)
+
+    barrier = pltpu.get_barrier_semaphore()
+    for way, cond in (("x", None), ("y", None), ("c", None), ("u", lambda: z < 3), ("d", lambda: z > 0)):
+        run_if(
+            cond,
+            lambda way=way: pl.semaphore_signal(
+                barrier, inc=1, device_id=net.peer[way], device_id_type=MESH
+            ),
+        )
 
     def own_cols(w):
         return pl.ds(pl.multiple_of(c * w, 128), w)
 
     cot_copy = pltpu.make_async_copy(cot_hbm.at[pl.ds(mp * IMGS, IMGS)], COT, local_sem.at[0])
-    cot_copy.start()
-    copies = [pltpu.make_async_copy(a_in, GA.at[0, y, dp, :, own_cols(D)], local_sem.at[1])]
-    for i in range(CHUNKS):
-        for j, w in enumerate((u_in, d_in)):
+    copies = []
+    first = 0
+    for i, (GM, w) in enumerate(zip(GMS, CHUNKS)):
+        for j, weight_in in enumerate((u_in, d_in)):
             copies.append(
                 pltpu.make_async_copy(
-                    w.at[:, pl.ds(CHUNK * i, CHUNK)],
-                    GM.at[i, j, y, dp, :, own_cols(CHUNK)],
-                    local_sem.at[2 + 2 * i + j],
+                    weight_in.at[:, pl.ds(first, w)],
+                    GM.at[j, y, dp, :, own_cols(w)],
+                    local_sem.at[1 + 2 * i + j],
                 )
             )
+        first += w
     for copy in copies:
         copy.start()
-    barrier = pltpu.get_barrier_semaphore()
-    for i in range(8):
-        for j in range(4):
-            @pl.when(jnp.logical_or(dp != i, mp != j))
-            def _():
-                pl.semaphore_signal(barrier, inc=1, device_id=(i, j), device_id_type=MESH)
+    patch_copy = pltpu.make_async_copy(patches, PIN, local_sem.at[7])
+    patch_copy.start()
+    cot_copy.start()
+
+    qkv = [qkv_in[i].astype(F32) for i in range(3)]
+    outs = out_in[...].astype(F32).T
+    low = lax.broadcasted_iota(jnp.int32, (96, 128), 1) < HEAD_DIM
+
+    def tail(v, high):
+        v = jnp.concatenate([v[:, 128:192], v[:, 128:192]], axis=1)
+        return v
+
+    tiles = [qkv[0][:, 0:128], qkv[1][:, 0:128], qkv[2][:, 0:128]]
+    tiles.append(jnp.where(low, tail(qkv[0], 0), tail(qkv[2], 1)))
+    tiles.append(jnp.where(low, tail(qkv[1], 0), tail(outs, 1)))
+    tiles.append(outs[:, 0:128])
+    GA[0, pl.ds(y, 1), pl.ds(dp, 1), :, own_cols(D)] = (
+        jnp.concatenate(tiles, axis=1).astype(BF16)[None, None]
+    )
 
     LOC[:, 0:PART] = master[...]
     lane = lax.broadcasted_iota(jnp.int32, (TASKS, PADP - PART), 1)
     LOC[:, PART:PADP] = jnp.where(
-        lane == 0, tasks[0, 0].astype(F32), jnp.where(lane == 1, tasks[1, 0].astype(F32), 0.0)
+        lane == 0, tasks[0, 0].astype(F32), jnp.where(lane == 1, tasks[0, 1].astype(F32), 0.0)
     )
     half = PADP // 2
     GP[0, pl.ds(y, 1), pl.ds(dp, 1), :, own_cols(half)] = (
@@ -321,30 +343,38 @@
     )
     for copy in copies:
         copy.wait()
-    pl.semaphore_wait(barrier, NDEV - 1)
+    inner = jnp.logical_and(z > 0, z < 3)
+    run_if(lambda: inner, lambda: pl.semaphore_wait(barrier, 5))
+    run_if(lambda: jnp.logical_not(inner), lambda: pl.semaphore_wait(barrier, 4))
 
     split = (32, 48, 64, 96)
-    ev = gather_events(net, GP, half, -0.5, (16, 16, 16, 16))
-    ev += gather_events(net, GA, D, 0.0, split)
-    for i in range(CHUNKS):
-        ev += gather_events(net, GM.at[i], CHUNK, 1.51 * (i + 1), split)
-    ev = [(-1 + 0.01 * k if f.__name__ == "start" else k, f) if hasattr(f, "__name__") else (k, f) for k, f in ev]
-    events = Events(ev)
-
-    g1 = gain_one[...]
-    g2 = gain_two[...]
+    gathers = [gather_events(net, GP, half, (16, 16, 16, 16)), gather_events(net, GA, D, split)]
+    gathers += [gather_events(net, GM, w, split) for GM, w in zip(GMS, CHUNKS)]
+    segments = [[gathers[i // 28][i % 28] for i in part] for part in ORDER]
+    position = [0]
+
+    def ahead(n=1):
+        position[0] += n
+        return segments[position[0] - n : position[0]]
+
+    def advance():
+        for f in ahead()[0]:
+            f()
+
+    g1 = gain_one[...].reshape(1, D)
+    g2 = gain_two[...].reshape(1, D)
     limits = [lengths[b] + LEAD for b in range(IMGS)]
     live = [
         (lax.broadcasted_iota(jnp.int32, (ROWS, 1), 0) < limits[b]).astype(F32) for b in range(IMGS)
     ]
 
-    events.run(0.5)
+    advance()
+    patch_copy.wait()
     for b in range(IMGS):
-        RES[b, LEAD:ROWS, :] = patches[b].astype(F32)
+        RES[b, LEAD:ROWS, :] = PIN[:, b, :].astype(F32)
     MACC[...] = jnp.zeros_like(MACC)
     GACC[...] = jnp.zeros_like(GACC)
-    SEND[...] = jnp.zeros_like(SEND)
-    events.run(6.11)
+    advance()
 
     task_rows = lax.broadcasted_iota(jnp.int32, (TASKS, 1), 0)
 
@@ -354,7 +384,7 @@
         low, high = raw[0:8], raw[8:16]
         rep, j = d // 16, d % 16
         for b in range(IMGS):
-            hot = (task_rows == tasks[b, 0]).astype(F32)
+            hot = (task_rows == tasks[0, b]).astype(F32)
             row = 2 * rep + b
             SEL[j, pl.ds(row, 1), 0:half] = jnp.sum(low * hot, axis=0, keepdims=True)
             SEL[j, pl.ds(row, 1), half:PADP] = jnp.sum(high * hot, axis=0, keepdims=True)
@@ -379,9 +409,9 @@
             for b in range(IMGS):
                 RES[b, 25 * rep + r : 25 * rep + r + 1, :] = seg[2 * rep + b : 2 * rep + b + 1]
 
+    advance()
     for b in range(IMGS):
         N1[b] = (norm_parts(RES[b])[0] * g1).astype(BF16)
-    events.run(6.61)
 
     def weight(ref, core, first, width, span):
         cols = pl.ds(pl.multiple_of(core * span + first, 128), width)
@@ -392,26 +422,23 @@
     wide = lax.broadcasted_iota(jnp.int32, (1, 640), 1)
     q_scale = jnp.where((wide < 128) | ((wide >= 384) & (wide < 448)), scale, 1.0)
 
-    def split_keys(first, step, n):
-        return [events.take(first + step * (j + 1)) for j in range(n)]
-
-    groups = split_keys(6.61, 0.15, 4)
+    groups = ahead(2)
 
     def project(t, _):
         at_step(t, groups)
-        w = weight(GA.at[0, t // 2], t % 2, 0, 640, D)
-        mixed = nn(N1[...].reshape(IMGS * ROWS, D), w).astype(BF16).astype(F32) * q_scale
-        QKV[t] = mixed.astype(BF16).reshape(IMGS, ROWS, 640)
+        for core in range(2):
+            w = weight(GA.at[0, t], core, 0, 640, D)
+            mixed = nn(N1[...].reshape(IMGS * ROWS, D), w) * q_scale
+            QKV[2 * t + core] = mixed.astype(BF16).reshape(IMGS, ROWS, 640)
         return 0
 
-    lax.fori_loop(0, 4, project, 0)
+    lax.fori_loop(0, 2, project, 0)
 
     key_rows = lax.broadcasted_iota(jnp.int32, (ROWS, ROWS), 0)
     zero = jnp.zeros((), BF16)
-    groups_a = split_keys(7.2, 0.15, 8)
-
-    def attend(t, _):
-        at_step(t, groups_a)
+    groups_a = ahead(ATT)
+
+    def attend(t):
         b, m = t // 4, t % 4
         tile = lambda i: QKV[m, b, :, 128 * i : 128 * i + 128]
         q01, k01, v01, q2v2, k2 = (tile(i) for i in range(5))
@@ -430,9 +457,14 @@
         CTX[b, :, pl.ds(pl.multiple_of(m * 256 + 128, 128), 128)] = keep(
             left, tn(p0, v01), tn(p1, v01)
         ).astype(BF16)
+
+    def attend_some(t, _):
+        at_step(t, groups_a)
+        for j in range(8 // ATT):
+            attend(t * (8 // ATT) + j)
         return 0
 
-    lax.fori_loop(0, 8, attend, 0)
+    lax.fori_loop(0, ATT, attend_some, 0)
 
     sums = [jnp.zeros((1, 1), F32) for _ in range(3)]
 
@@ -440,7 +472,7 @@
         return jnp.sum(jnp.sum(v, axis=0, keepdims=True), axis=1, keepdims=True)
 
     for b in range(IMGS):
-        events.run(8.4 + 0.2 * (b + 1))
+        advance()
         attn = jnp.zeros((ROWS, D), F32)
         for m in range(4):
             attn += nt(CTX[b, :, 256 * m : 256 * m + 256], weight(GA.at[0, m // 2], m % 2, 512, 256, D))
@@ -450,155 +482,195 @@
         N2[b] = (norm_parts(res2)[0] * g2).astype(BF16)
     cot_copy.wait()
 
-    done = [1.51 * (i + 1) + 6.61 for i in range(CHUNKS)]
-    groups_m = [[], [], [], [], [], []]
-    for i in range(CHUNKS):
-        groups_m[2 * i] = events.take(done[i])
-        groups_m[2 * i + 1] = events.take(done[i] + 0.6)
-
-    def feed(t, _):
-        at_step(t, groups_m)
-        i, yy = t // 2, t % 2
+    def feed(i, yy):
+        GM, w = GMS[i], CHUNKS[i]
         rows2 = N2[...].reshape(IMGS * ROWS, D)
         cot = COT[...].reshape(IMGS * ROWS, D)
         for core in range(2):
-            up = nn(rows2, weight(GM.at[i, 0, yy], core, 0, CHUNK, CHUNK))
-            back = nn(cot, weight(GM.at[i, 1, yy], core, 0, CHUNK, CHUNK))
+            up = nn(rows2, weight(GM.at[0, yy], core, 0, w, w))
+            back = nn(cot, weight(GM.at[1, yy], core, 0, w, w))
             cumul = 0.5 * (1.0 + lax.erf(up * 0.7071067811865476))
             density = jnp.exp(-0.5 * up * up) * 0.3989422804014327
-            ACT[:, CHUNK * core : CHUNK * (core + 1)] = (up * cumul).astype(BF16)
-            GU[:, CHUNK * core : CHUNK * (core + 1)] = (back * (cumul + up * density)).astype(BF16)
-        wide_d = weight(GM.at[i, 1, yy], 0, 0, 2 * CHUNK, CHUNK)
-        MACC[...] += nt(ACT[...], wide_d).reshape(IMGS, ROWS, D)
-        wide_u = weight(GM.at[i, 0, yy], 0, 0, 2 * CHUNK, CHUNK)
-        GACC[...] += nt(GU[...], wide_u).reshape(IMGS, ROWS, D)
+            ACT[:, w * core : w * (core + 1)] = (up * cumul).astype(BF16)
+            GU[:, w * core : w * (core + 1)] = (back * (cumul + up * density)).astype(BF16)
+        MACC[...] += nt(ACT[:, 0 : 2 * w], weight(GM.at[1, yy], 0, 0, 2 * w, w)).reshape(IMGS, ROWS, D)
+        GACC[...] += nt(GU[:, 0 : 2 * w], weight(GM.at[0, yy], 0, 0, 2 * w, w)).reshape(IMGS, ROWS, D)
+
+    for i in range(len(CHUNKS)):
+        groups_m = ahead(2)
+
+        def step(t, _, i=i, groups_m=groups_m):
+            at_step(t, groups_m)
+            feed(i, t)
+            return 0
+
+        lax.fori_loop(0, 2, step, 0)
+    advance()
+
+    for b in range(IMGS):
+        g = COT[b].astype(F32) + norm_back(RES2[b], g2, GACC[b])
+        G2[b] = g
+        G2B[b] = g.astype(BF16)
+
+    def context_back(m, _):
+        cols = pl.ds(pl.multiple_of((m % 2) * D + 512, 128), 256)
+        w = GA[0, m // 2, :, :, cols].reshape(D, 256)
+        DC[m] = nn(G2B[...].reshape(IMGS * ROWS, D), w).astype(BF16).reshape(IMGS, ROWS, 256)
         return 0
 
-    lax.fori_loop(0, 2 * CHUNKS, feed, 0)
-    events.run(1e9)
-
+    lax.fori_loop(0, 4, context_back, 0, unroll=4)
+
+    def attend_back(b):
+        tiles, grad_probs, grad_scores = [], [], []
+        for m in range(4):
+            tiles.append(
+                [QKV[m, b, :, 128 * i : 128 * i + 128] for i in range(5)]
+                + [DC[m, b, :, 0:128], DC[m, b, :, 128:256]]
+            )
+            q01, k01, v01, q2v2, k2, c2, c01 = tiles[m]
+            grad_probs.append(
+                [nt(keep(left, v01, zero), c01), nt(keep(left, zero, v01), c01), nt(keep(left, zero, q2v2), c2)]
+            )
+        for m in range(4):
+            out = []
+            for h in range(3):
+                pf, dp_ = PT[4 * b + m, h].astype(F32), grad_probs[m][h]
+                inner = jnp.sum(pf * dp_, axis=0, keepdims=True)
+                out.append((pf * (dp_ - inner)).astype(BF16))
+            grad_scores.append(out)
+        for m in range(4):
+            q01, k01, v01, q2v2, k2, c2, c01 = tiles[m]
+            s0, s1, s2 = grad_scores[m]
+            p0, p1, p2 = (PT[4 * b + m, h] for h in range(3))
+            DM[m, b, :, 0:128] = (keep(left, tn(s0, k01), tn(s1, k01)) * scale).astype(BF16)
+            DM[m, b, :, 128:256] = keep(left, nn(s0, q01), nn(s1, q01)).astype(BF16)
+            DM[m, b, :, 256:384] = keep(left, nn(p0, c01), nn(p1, c01)).astype(BF16)
+            DM[m, b, :, 384:512] = keep(left, tn(s2, k2) * scale, nn(p2, c2)).astype(BF16)
+            DM[m, b, :, 512:640] = keep(left, nn(s2, q2v2), 0.0).astype(BF16)
+
+    def grad_rows(b, first, last):
+        grad = jnp.zeros((last - first, D), F32)
+        for m in range(4):
+            grad += nt(DM[m, b, first:last], weight(GA.at[0, m // 2], m % 2, 0, 640, D))
+        GACC[b, first:last] = G2[b, first:last] + norm_back(RES[b, first:last], g1, grad)
+
+    def swap(k, src, dst, sems):
+        other = lax.rem(device + k, NDEV)
+        pltpu.make_async_remote_copy(
+            src_ref=src(other),
+            dst_ref=dst,
+            send_sem=all_sem.at[sems],
+            recv_sem=all_sem.at[sems + 1],
+            device_id=(other // 4, lax.rem(other, 4)),
+            device_id_type=MESH,
+        ).start()
+
+    wide = lax.broadcasted_iota(jnp.int32, (2, PADP), 1)
+
+    def to_owners(b):
+        for rep in range(2):
+            LEADR[:, rep : rep + 1, :] = GACC[b, 25 * rep : 25 * rep + 25, :][:, None, :]
+        for q in range(16):
+            r, off = (PART * q) // D, (PART * q) % D
+            msg, have = None, -off
+            while have < PART:
+                row = LEADR[r]
+                moved = pltpu.roll(row, have % D, 1) if have % D else row
+                moved = jnp.concatenate([moved, moved[:, 0 : PADP - D]], axis=1)
+                msg = moved if msg is None else jnp.where(wide < have, msg, moved)
+                have += D
+                r += 1
+            msg = jnp.where(wide < PART, msg, 0.0).astype(BF16)
+            for rep in range(2):
+                SEND[b, 16 * rep + q] = jnp.concatenate(
+                    [msg[rep : rep + 1, 0:half], msg[rep : rep + 1, half:PADP]], axis=0
+                )
+        for k in range(1, NDEV):
+            swap(k, lambda other: SEND.at[b, other], RECV.at[b, device], 2 * b)
+        RECV[b, pl.ds(device, 1)] = SEND[b, pl.ds(device, 1)]
+
+    def others(ref):
+        return ref.at[pl.ds(0, NDEV - 1)]
+
+    def wait_all(ref, sem):
+        pltpu.make_async_copy(others(ref), others(ref), all_sem.at[sem]).wait()
+
+    attend_back(0)
+    grad_rows(0, 0, ROWS)
+    to_owners(0)
+    attend_back(1)
+    some = 64
+    grad_rows(1, 0, some)
+    to_owners(1)
+
+    grad_rows(1, some, ROWS)
     for b in range(IMGS):
         mlp = MACC[b]
         block = RES2[b] + mlp
-        out_block[b] = block.astype(BF16)
+        BOUT[b] = block.astype(BF16)
         sums[0] += total(block * block * live[b])
         sums[2] += total(mlp * mlp * live[b])
-        g = COT[b].astype(F32) + norm_back(RES2[b], g2, GACC[b])
-        MACC[b] = g
-        G2B[b] = g.astype(BF16)
-
-    def attend_back(t, _):
-        b, m = t // 4, t % 4
-        tile = lambda i: QKV[m, b, :, 128 * i : 128 * i + 128]
-        q01, k01, v01, q2v2, k2 = (tile(i) for i in range(5))
-        cols = pl.ds(pl.multiple_of((m % 2) * D + 512, 128), 256)
-        w = GA[0, m // 2, :, :, cols].reshape(D, 256)
-        dctx = nn(G2B[b], w).astype(BF16)
-        c2, c01 = dctx[:, 0:128], dctx[:, 128:256]
-
-        def back(p, v, grad):
-            pf = p.astype(F32)
-            dp_ = nt(v, grad)
-            inner = jnp.sum(pf * dp_, axis=0, keepdims=True)
-            return (pf * (dp_ - inner)).astype(BF16)
-
-        p0, p1, p2 = PT[t, 0], PT[t, 1], PT[t, 2]
-        s0 = back(p0, keep(left, v01, zero), c01)
-        s1 = back(p1, keep(left, zero, v01), c01)
-        s2 = back(p2, keep(left, zero, q2v2), c2)
-        DM[m, b, :, 0:128] = (keep(left, tn(s0, k01), tn(s1, k01)) * scale).astype(BF16)
-        DM[m, b, :, 128:256] = keep(left, nn(s0, q01), nn(s1, q01)).astype(BF16)
-        DM[m, b, :, 256:384] = keep(left, nn(p0, c01), nn(p1, c01)).astype(BF16)
-        DM[m, b, :, 384:512] = keep(left, tn(s2, k2) * scale, nn(p2, c2)).astype(BF16)
-        DM[m, b, :, 512:640] = keep(left, nn(s2, q2v2), 0.0).astype(BF16)
-        return 0
-
-    lax.fori_loop(0, 8, attend_back, 0)
-
-    for b in range(IMGS):
-        grad = jnp.zeros((ROWS, D), F32)
-        for m in range(4):
-            grad += nt(DM[m, b], weight(GA.at[0, m // 2], m % 2, 0, 640, D))
-        grad = MACC[b] + norm_back(RES[b], g1, grad)
-        GACC[b] = grad
-        out_patch[b] = GACC[b, LEAD:ROWS, :].astype(BF16)
-
-    for rep in range(2):
-        for b in range(IMGS):
-            LEADR[:, 2 * rep + b : 2 * rep + b + 1, :] = GACC[b, 25 * rep : 25 * rep + 25, :][:, None, :]
-    wide = lax.broadcasted_iota(jnp.int32, (4, PADP), 1)
-    for q in range(16):
-        r, off = (PART * q) // D, (PART * q) % D
-        msg, have = None, -off
-        while have < PART:
-            row = jnp.concatenate([LEADR[r, 0:4, :], jnp.zeros((4, PADP - D), F32)], axis=1)
-            moved = pltpu.roll(row, have % PADP, 1) if have % PADP else row
-            msg = moved if msg is None else jnp.where(wide < have, msg, moved)
-            have += D
-            r += 1
-        msg = jnp.where(wide < PART, msg, 0.0)
-        SEND[q] = msg[0:2]
-        SEND[16 + q] = msg[2:4]
-
-    def swap(d, what, start):
-        i, j = d // 4, d % 4
-
-        @pl.when(d != device)
-        def _():
-            pltpu.make_async_remote_copy(
-                src_ref=what(d, True),
-                dst_ref=what(device, False),
-                send_sem=all_sem.at[2 * start],
-                recv_sem=all_sem.at[2 * start + 1],
-                device_id=(i, j),
-                device_id_type=MESH,
-            ).start()
-
-    def to_owner(d, _):
-        swap(d, lambda k, mine: SEND.at[k] if mine else RECV.at[k], 0)
-        return 0
-
-    lax.fori_loop(0, NDEV, to_owner, 0)
-    RECV[pl.ds(device, 1)] = SEND[pl.ds(device, 1)]
-    others = RECV.at[pl.ds(0, NDEV - 1)]
-    pltpu.make_async_copy(others, others, all_sem.at[1]).wait()
-
-    def add(s, acc):
-        acc = acc + jnp.concatenate([ONEHOT[s, 0]] * (PADP // 128), axis=1) * RECV[s, 0:1, :]
-        return acc + jnp.concatenate([ONEHOT[s, 1]] * (PADP // 128), axis=1) * RECV[s, 1:2, :]
-
-    task_grad = lax.fori_loop(0, NDEV, add, jnp.zeros((TASKS, PADP), F32))
-    square = total(task_grad * task_grad)
-    lane = lax.broadcasted_iota(jnp.int32, (8, 128), 1)
+    block_copy = pltpu.make_async_copy(BOUT, out_block, local_sem.at[8])
+    block_copy.start()
+
+    def add_image(b, acc):
+        wait_all(RECV.at[b], 2 * b + 1)
+
+        def add(s, acc):
+            rows = RECV[b, s].astype(F32)
+            hot = jnp.concatenate([ONEHOT[s, b]] * (half // 128), axis=1)
+            return acc[0] + hot * rows[0:1], acc[1] + hot * rows[1:2]
+
+        return lax.fori_loop(0, NDEV, add, acc, unroll=8)
+
+    acc = (jnp.zeros((TASKS, half), F32), jnp.zeros((TASKS, half), F32))
+    acc = add_image(1, add_image(0, acc))
+    square = total(acc[0] * acc[0]) + total(acc[1] * acc[1])
+    lane = lax.broadcasted_iota(jnp.int32, (1, 128), 1)
     count = (limits[0] + limits[1]).astype(F32)
-    stats = jnp.where(lane == 0, square, jnp.where(lane == 1, sums[0], jnp.where(lane == 2, sums[1], jnp.where(
-        lane == 3, sums[2], jnp.where(lane == 4, count, 0.0)))))
+    stats = jnp.zeros((1, 128), F32)
+    for i, v in enumerate((square, sums[0], sums[1], sums[2], count)):
+        stats = jnp.where(lane == i, v, stats)
     STSUM[...] = stats
     SREC[pl.ds(device, 1)] = stats[None]
-
-    def to_all(d, _):
-        swap(d, lambda k, mine: STSUM if mine else SREC.at[k], 1)
-        return 0
-
-    lax.fori_loop(0, NDEV, to_all, 0)
-    out_task[...] = task_grad[:, 0:PART]
-    others2 = SREC.at[pl.ds(0, NDEV - 1)]
-    pltpu.make_async_copy(others2, others2, all_sem.at[3]).wait()
+    for k in range(1, NDEV):
+        swap(k, lambda other: STSUM, SREC.at[device], 4)
+
+    out_task[...] = jnp.concatenate(acc, axis=1)[:, 0:PART]
+    for b in range(IMGS):
+        PAIR[:, b : b + 1, :] = GACC[b, LEAD:ROWS, :][:, None, :]
+    PIN[...] = PAIR[...].astype(BF16)
+    patch_out = pltpu.make_async_copy(PIN, out_patch, local_sem.at[9])
+    patch_out.start()
+    for b in range(IMGS):
+        wait_all(RECV.at[b], 2 * b)
+    net.finish()
+    block_copy.wait()
+    wait_all(SREC, 5)
     out_stats[...] = jnp.sum(SREC[...], axis=0)
-    pltpu.make_async_copy(others, others, all_sem.at[0]).wait()
-    pltpu.make_async_copy(others2, others2, all_sem.at[2]).wait()
-    net.finish()
+    wait_all(SREC, 4)
+    patch_out.wait()
 
 
 def update_kernel(
     task_grad, stats, master, first_moment, second_moment, block_in, patch_in,
-    out_grad, out_first, out_second, out_master, out_copy, out_small, block_out, patch_out,
+    out_grad, out_first, out_second, out_master, out_copy, out_norm, out_rms, block_out, patch_out,
+    block_held, patch_held, sem,
 ):
-    block_out[...] = block_in[...]
-    patch_out[...] = patch_in[...]
+    inward = [
+        pltpu.make_async_copy(block_in.at[0], block_held.at[0], sem.at[0]),
+        pltpu.make_async_copy(block_in.at[1], block_held.at[1], sem.at[1]),
+        pltpu.make_async_copy(patch_in, patch_held, sem.at[2]),
+    ]
+    outward = [
+        pltpu.make_async_copy(block_held.at[0], block_out.at[0], sem.at[3]),
+        pltpu.make_async_copy(block_held.at[1], block_out.at[1], sem.at[4]),
+        pltpu.make_async_copy(patch_held, patch_out, sem.at[5]),
+    ]
+    for copy in inward:
+        copy.start()
     st = stats[0:1, :]
-    square = st[0:1, 0:1]
-    norm = jnp.sqrt(square)
+    norm = jnp.sqrt(st[0:1, 0:1])
     grad = task_grad[...] * (clip_level / jnp.maximum(norm, clip_level))
     first = beta_one * first_moment[...] + (1.0 - beta_one) * grad
     second = beta_two * second_moment[...] + (1.0 - beta_two) * grad * grad
@@ -612,21 +684,21 @@
     out_second[...] = second
     out_master[...] = new
     out_copy[...] = new.astype(BF16)
-    lane = lax.broadcasted_iota(jnp.int32, (1, 128), 1)
-    inside = jnp.where(lane == 0, square, st / (st[0:1, 4:5] * D))
-    out_small[...] = jnp.sqrt(inside)
+    out_norm[0] = norm[0, 0]
+    rms = jnp.sqrt(st / (st[0:1, 4:5] * D))
+    for i in range(3):
+        out_rms[i] = rms[0, i + 1]
+    for copy, after in zip(inward, outward):
+        copy.wait()
+        after.start()
+    for copy in outward:
+        copy.wait()
 
 
 def fast_body(
     patches, lengths, tasks, prompt_master, first_moment, second_moment,
     gain_one, gain_two, w_qkv, w_out, w_up, w_down, cotangent,
 ):
-    heads = w_qkv.reshape(96, 3, 3, HEAD_DIM)
-    outs = w_out.T.reshape(96, 3, HEAD_DIM)
-    order = [heads[:, 0, 0], heads[:, 0, 1], heads[:, 1, 0], heads[:, 1, 1], heads[:, 2, 0], heads[:, 2, 1],
-             heads[:, 0, 2], heads[:, 2, 2], heads[:, 1, 2], outs[:, 2], outs[:, 0], outs[:, 1]]
-    a_in = jnp.concatenate(order, axis=1)
-    d_in = w_down.T
     vmem = pl.BlockSpec(memory_space=pltpu.VMEM)
     smem = pl.BlockSpec(memory_space=pltpu.SMEM)
     anywhere = pl.BlockSpec(memory_space=pl.ANY)
@@ -635,16 +707,18 @@
         layer_kernel,
         out_shape=[
             jax.ShapeDtypeStruct((IMGS, ROWS, D), BF16),
-            jax.ShapeDtypeStruct((IMGS, PATCH, D), BF16),
+            jax.ShapeDtypeStruct((PATCH, IMGS, D), BF16),
             jax.ShapeDtypeStruct((TASKS, PART), F32),
-            jax.ShapeDtypeStruct((8, 128), F32),
+            jax.ShapeDtypeStruct((1, 128), F32),
         ],
-        in_specs=[vmem, smem, smem, vmem, vmem, vmem, vmem, vmem, vmem, anywhere],
-        out_specs=[vmem] * 4,
+        in_specs=[anywhere, smem, smem, vmem, vmem, vmem, vmem, vmem, anywhere, anywhere, anywhere],
+        out_specs=[anywhere] * 2 + [vmem] * 2,
         scratch_shapes=[
             V((1, 2, 8, 16, PADP), BF16),
             V((1, 2, 8, 96, 2 * D), BF16),
-            V((CHUNKS, 2, 2, 8, 96, 2 * CHUNK), BF16),
+            V((2, 2, 8, 96, 2 * CHUNKS[0]), BF16),
+            V((2, 2, 8, 96, 2 * CHUNKS[1]), BF16),
+            V((2, 2, 8, 96, 2 * CHUNKS[2]), BF16),
             V((TASKS, PADP), F32),
             V((16, 4, PADP), F32),
             V((IMGS, ROWS, D), F32),
@@ -655,40 +729,53 @@
             V((IMGS, ROWS, D), F32),
             V((IMGS, ROWS, D), BF16),
             V((IMGS, ROWS, D), BF16),
-            V((IMGS * ROWS, 2 * CHUNK), BF16),
-            V((IMGS * ROWS, 2 * CHUNK), BF16),
+            V((IMGS * ROWS, 2 * CHUNKS[0]), BF16),
+            V((IMGS * ROWS, 2 * CHUNKS[0]), BF16),
+            V((IMGS, ROWS, D), F32),
             V((IMGS, ROWS, D), F32),
             V((IMGS, ROWS, D), F32),
             V((IMGS, ROWS, D), BF16),
             V((4, IMGS, ROWS, 640), BF16),
-            V((25, 4, D), F32),
-            V((NDEV, IMGS, PADP), F32),
-            V((NDEV, IMGS, PADP), F32),
+            V((4, IMGS, ROWS, 256), BF16),
+            V((25, 2, D), F32),
+            V((PATCH, IMGS, D), F32),
+            V((PATCH, IMGS, D), BF16),
+            V((IMGS, ROWS, D), BF16),
+            V((IMGS, NDEV, 2, PADP // 2), BF16),
+            V((IMGS, NDEV, 2, PADP // 2), BF16),
             V((NDEV, IMGS, TASKS, 128), F32),
-            V((NDEV, 8, 128), F32),
-            V((8, 128), F32),
-            pltpu.SemaphoreType.DMA((8,)),
+            V((NDEV, 1, 128), F32),
+            V((1, 128), F32),
+            pltpu.SemaphoreType.DMA((10,)),
             pltpu.SemaphoreType.DMA((RING,)),
-            pltpu.SemaphoreType.DMA((21 * (2 + CHUNKS),)),
-            pltpu.SemaphoreType.DMA((4,)),
+            pltpu.SemaphoreType.DMA((13 + 21 * (1 + len(CHUNKS)),)),
+            pltpu.SemaphoreType.DMA((6,)),
         ],
         compiler_params=pltpu.CompilerParams(
             collective_id=0, has_side_effects=True, vmem_limit_bytes=58 << 20
         ),
-    )(patches, lengths, tasks, prompt_master, gain_one[None, :], gain_two[None, :], a_in, w_up, d_in, cotangent)
-    grad, first, second, master, copy, small, block_out, patch_out = pl.pallas_call(
+    )(
+        patches.transpose(1, 0, 2), lengths, tasks.T, prompt_master, gain_one, gain_two,
+        w_qkv.transpose(1, 0, 2), w_out, w_up, w_down.T, cotangent,
+    )
+    state = jax.ShapeDtypeStruct((TASKS, PART), F32)
+    grad, first, second, master, copy, norm, rms, block_out, patch_out = pl.pallas_call(
         update_kernel,
-        out_shape=[jax.ShapeDtypeStruct((TASKS, PART), F32)] * 4
+        out_shape=[state] * 4
         + [
             jax.ShapeDtypeStruct((TASKS, PART), BF16),
-            jax.ShapeDtypeStruct((1, 128), F32),
+            jax.ShapeDtypeStruct((1,), F32),
+            jax.ShapeDtypeStruct((3,), F32),
             jax.ShapeDtypeStruct((IMGS, ROWS, D), BF16),
-            jax.ShapeDtypeStruct((IMGS, PATCH, D), BF16),
+            jax.ShapeDtypeStruct((PATCH, IMGS, D), BF16),
         ],
-        in_specs=[vmem] * 7,
-        out_specs=[vmem] * 8,
+        in_specs=[vmem] * 5 + [anywhere] * 2,
+        out_specs=[vmem] * 5 + [smem] * 2 + [anywhere] * 2,
+        scratch_shapes=[V((IMGS, ROWS, D), BF16), V((PATCH, IMGS, D), BF16), pltpu.SemaphoreType.DMA((6,))],
     )(task, stats, prompt_master, first_moment, second_moment, block, patch)
-    return block_out, patch_out, grad, small[0, 0], first, second, master, copy, small[0, 1:4]
+    return (
+        block_out, patch_out.transpose(1, 0, 2), grad, norm.reshape(()), first, second, master, copy, rms,
+    )
 
 
 def layer_norm(values, gain):

time: 127 us -> 96.1 us (0.76)
  Pallas kernels: 112 us -> 95.1 us
  local copies, waits for them, and re-layouts: 13.4 us -> 0 us
    pallas_call x1, Pallas kernels: 109 us -> 91.4 us  [fast_body(): pl.pallas_call(layer_kernel, out_shape=[jax.ShapeDtypeStruct((IMGS, ROWS,...]
    unnamed x16 -> x0, local copies, waits for them, and re-layouts: 8.04 us -> none
    broadcast_in_dim x2 -> x0, local copies, waits for them, and re-layouts: 2.53 us -> none  [the longest x1 1.27 us: fast_body(): gain_one[None, :]]
where the time goes in v2:
time: 96.1 us; the launch traced here: 95.9 us
  Pallas kernels  95.1 us (99%)
    pallas_call x1, Pallas kernels, fast_body(): pl.pallas_call(layer_kernel, out_shape=[jax.ShapeDtypeStruct((IMGS, ROWS,...  91.4 us
    pallas_call x1, Pallas kernels, fast_body(): pl.pallas_call(update_kernel, out_shape=[state] * 4 + [jax.ShapeDtypeStru...  3.72 us

profile of v2, /device:TPU:0, one launch (start us, length us, event | category | flops | bytes accessed | tf_op | source)
XLA Modules:
  0.0 95.9 jit_solution(17989421460576317136)
XLA Ops:
  0.6 91.4 %shard_map.196 = (bf16[2,256,768]{2,1,0:T(8,128)(2,1)}, bf16[206,2,768]{2,1,0:T(2,128)(2,1)}, f32[8,1200]{1,0:T(8,128)}, f32[1,128]{1,0:T(1,128)}) custom-call(bf16[206,2,768]{2,1,0:T(2,128)(2,1)} %bitcast.6, s32[2]{0:T(128)} %lengths.1, s32[1,2]{1,0:T(1,128)} %bitcast.9, f32[8,1200]{1,0:T(8,128)} %master.3, f32[768]{0:T(1024)} %gain_one.1, f32[768]{0:T(1024)} %gain_two.1, ...), custom_call_target="tpu_custom_call" | custom-call | tf_op jit(solution)/shard_map/pallas_call | solution.py:706
  92.0 3.7 %shard_map.197 = (f32[8,1200]{1,0:T(8,128)}, f32[8,1200]{1,0:T(8,128)}, f32[8,1200]{1,0:T(8,128)}, f32[8,1200]{1,0:T(8,128)}, bf16[8,1200]{1,0:T(8,128)(2,1)}, /...) custom-call(f32[8,1200]{1,0:T(8,128)} %get-tuple-element.22.task_grad, ...), custom_call_target="tpu_custom_call" | custom-call | tf_op jit(solution)/shard_map/pallas_call | solution.py:762

commit v3 on v2

--- a/solution.py
+++ b/solution.py
@@ -31,29 +31,18 @@
 PART = 1200
 PADP = 1280
 NDEV = 32
-CHUNKS = (256, 256, 256)
+DOWNS = (384, 384)
+UPS = (384, 384)
+SPLITS = ((16, 48, 64, 96), (32, 48, 80, 96), (16, 48, 64, 96), (32, 48, 80, 96), (16, 48, 64, 96))
 ORDER = (
-    (0, 28, 112, 84, 56, 4, 32, 37, 44,),
-    (13, 17, 16, 60, 72, 14, 18, 48, 41, 38, 65, 20, 45, 22, 15, 21, 93, 19, 42, 46, 52, 39, 23, 69, 26, 25, 66, 73, 27, 24,),
-    (49, 88,),
-    (43, 47, 67, 94, 70, 121, 53, 50, 100, 74, 51, 95, 54, 97, 101, 116, 55,),
-    (71, 128, 76, 75,),
-    (77, 98, 122, 104,),
-    (102,),
-    (125, 129, 105, 108,),
-    (78, 80, 79, 132,),
-    (123,),
-    (81, 99, 103, 83,),
-    (126, 130, 109, 82, 136, 106,),
-    (127, 131, 107,),
-    (110, 133, 111, 134,),
-    (137, 135,),
-    (138, 139,),
-    (),
-    (),
+    0, 28, 56, 84, 1000, 4, 16, 32, 37, 60, 44, 13, 17, 72, 41, 112, 38, 45, 20, 14,
+    18, 65, 48, 42, 46, 15, 19, 39, 69, 49, 140, 66, 21, 76, 121, 73, 116, 22, 43, 47,
+    23, 93, 70, 128, 88, 27, 50, 1001, 149, 67, 100, 122, 51, 1002, 125, 74, 71, 75, 55, 144,
+    1003, 97, 156, 1004, 94, 1005, 123, 150, 126, 129, 130, 1006, 1007, 153, 98, 101, 1008, 95, 151, 78,
+    77, 1009, 127, 79, 131, 1010, 157, 132, 133, 134, 154, 102, 83, 1011, 1013, 99, 103, 1014, 135, 160,
+    104, 1012, 158, 139, 1017, 155, 105, 161, 159, 1018, 106, 1019, 107, 162, 1020, 163, 111, 1015, 1016, 167,
+    1021, 1022, 1023, 1024,
 )
-RING = 24
-ATT = 4
 
 
 def run_if(cond, f):
@@ -63,24 +52,10 @@
         pl.when(cond())(f)
 
 
-def both(*conds):
-    conds = [c for c in conds if c is not None]
-    if not conds:
-        return None
-
-    def value():
-        out = conds[0]()
-        for c in conds[1:]:
-            out = jnp.logical_and(out, c())
-        return out
-
-    return value
-
-
 class Net:
     def __init__(self, send_sem, recv_sem):
         self.send_sem, self.recv_sem = send_sem, recv_sem
-        self.sent = self.used = 0
+        self.sends = self.recvs = 0
         dp, mp = lax.axis_index("dp"), lax.axis_index("mp")
         z, x, y, c = dp // 2, dp % 2, mp // 2, mp % 2
         self.z, self.x, self.y, self.c = z, x, y, c
@@ -92,152 +67,139 @@
             "u": (jnp.minimum(2 * z + 2 + x, 6 + x), mp),
             "d": (jnp.maximum(2 * z - 2 + x, x), mp),
         }
-        self.ring = [None] * RING
-
-    def alloc(self, n):
-        first = self.used
-        self.used += n
-        return first
-
-    def send(self, way, view, sem, cond=None):
-        i = self.sent % RING
-        self.sent += 1
-        if self.ring[i] is not None:
-            self.wait_sent(i)
-
-        def copy():
-            v = view()
-            return pltpu.make_async_remote_copy(
-                src_ref=v,
-                dst_ref=v,
-                send_sem=self.send_sem.at[i],
-                recv_sem=self.recv_sem.at[sem()],
-                device_id=self.peer[way],
-                device_id_type=MESH,
-            )
-
-        run_if(cond, lambda: copy().start())
-        self.ring[i] = (cond, copy)
-
-    def wait_sent(self, i):
-        cond, copy = self.ring[i]
-        run_if(cond, lambda: copy().wait_send())
-        self.ring[i] = None
-
-    def recv(self, view, sem, cond=None):
-        def wait():
-            v = view()
-            pltpu.make_async_copy(v, v, self.recv_sem.at[sem()]).wait()
-
-        run_if(cond, wait)
-
-    def finish(self):
-        for i in range(RING):
-            if self.ring[i] is not None:
-                self.wait_sent(i)
+
+    def send(self, way, view, sem, landed):
+        pltpu.make_async_remote_copy(
+            src_ref=view,
+            dst_ref=view,
+            send_sem=self.send_sem.at[sem],
+            recv_sem=self.recv_sem.at[landed],
+            device_id=self.peer[way],
+            device_id_type=MESH,
+        ).start()
+
+    def recv(self, view, landed):
+        pltpu.make_async_copy(view, view, self.recv_sem.at[landed]).wait()
+
+    def wait_sent(self, view, sem):
+        pltpu.make_async_copy(view, view, self.send_sem.at[sem]).wait()
 
 
 def gather_events(net, G, W, split):
     z, x, y, c = net.z, net.x, net.y, net.c
     r1, r2, r3, rows = split
     some = 4 if r3 > r1 else 0
-    f_sem, zs_sem, zp_sem, m_sem, l_sem, c_sem = (net.alloc(n) for n in (1, some, 4, some, 4, 4))
-    not_top, not_low = (lambda: z < 3), (lambda: z > 0)
+    f_sem = net.recvs
+    zs_sem, zp_sem, m_sem = f_sem + 1, f_sem + 1 + some, f_sem + 5 + some
+    l_sem, c_sem = f_sem + 5 + 2 * some, f_sem + 9 + 2 * some
+    net.recvs = c_sem + 1
+    start_sent, single_sent, pair_sent, middle_sent, last_sent, core_sent = range(net.sends, net.sends + 6)
+    net.sends += 6
     every = slice(None)
+    ends = r1 + rows - r3
 
     def V(yy, d, first, last, other=False):
-        def view():
-            core = (1 - c) if other else c
-            cols = pl.ds(pl.multiple_of(core * W, 128), W)
-            return G.at[:, yy, d() if callable(d) else d, pl.ds(first, last - first), cols]
-
-        return view
+        core = (1 - c) if other else c
+        cols = pl.ds(pl.multiple_of(core * W, 128), W)
+        return G.at[:, yy, d, pl.ds(first, last - first), cols]
 
     def two(p):
-        return lambda: pl.ds(2 * p(), 2)
+        return pl.ds(2 * p, 2)
 
     def one(p):
-        return lambda: 2 * p() + x
-
-    def at(sem, p):
-        return lambda: sem + p()
-
-    own = lambda: z
-
-    def send(way, yy, d, first, last, sem, cond=None):
+        return 2 * p + x
+
+    def send(way, yy, d, first, last, sem, landed):
         if last > first:
-            net.send(way, V(yy, d, first, last), sem, cond)
-
-    def planes(k):
+            net.send(way, V(yy, d, first, last), sem, landed)
+
+    def sides(k, f):
         if k == 0:
-            return [(own, None)]
-        return [(lambda: z - k, lambda: z >= k), (lambda: z + k, lambda: z + k <= 3)]
-
-    def middle(p, cond):
-        send("x", y, one(p), r1, r2, at(m_sem, p), cond)
-        send("y", y, one(p), r2, r3, at(m_sem, p), cond)
+            f(z, None, None)
+        else:
+            pl.when(z >= k)(lambda: f(z - k, "u", z < 3))
+            pl.when(z + k <= 3)(lambda: f(z + k, "d", z > 0))
+
+    def middle(p):
+        send("x", y, one(p), r1, r2, middle_sent, m_sem + p)
+        send("y", y, one(p), r2, r3, middle_sent, m_sem + p)
 
     def start():
-        send("x", y, one(own), 0, r1, lambda: f_sem)
-        send("y", y, one(own), r3, rows, lambda: f_sem)
-        send("u", y, one(own), r1, r3, at(zs_sem, own), not_top)
-        send("d", y, one(own), r1, r3, at(zs_sem, own), not_low)
-        middle(own, None)
-
-    def pair(way, p, cond):
-        send(way, y, two(p), 0, r1, at(zp_sem, p), cond)
-        send(way, every, one(p), r3, rows, at(zp_sem, p), cond)
+        send("x", y, one(z), 0, r1, start_sent, f_sem)
+        send("y", y, one(z), r3, rows, start_sent, f_sem)
+        if r3 > r1:
+            pl.when(z < 3)(lambda: send("u", y, one(z), r1, r3, single_sent, zs_sem + z))
+            pl.when(z > 0)(lambda: send("d", y, one(z), r1, r3, single_sent, zs_sem + z))
+            middle(z)
+
+    def pair(way, p):
+        send(way, y, two(p), 0, r1, pair_sent, zp_sem + p)
+        send(way, every, one(p), r3, rows, pair_sent, zp_sem + p)
 
     def first_hop():
-        net.recv(V(y, one(own), 0, r1 + rows - r3), lambda: f_sem)
-        pair("u", own, not_top)
-        pair("d", own, not_low)
-
-    def ways(k):
-        return [(p, cond, w, far) for (p, cond), w, far in zip(planes(k), "ud", (not_top, not_low))]
+        net.recv(V(y, one(z), 0, ends), f_sem)
+        pl.when(z < 3)(lambda: pair("u", z))
+        pl.when(z > 0)(lambda: pair("d", z))
 
     def single_hop(k):
-        for p, cond, way, far in ways(k):
-            net.recv(V(y, one(p), r1, r3), at(zs_sem, p), cond)
+        def hop(p, way, more):
+            net.recv(V(y, one(p), r1, r3), zs_sem + p)
             if k < 3:
-                send(way, y, one(p), r1, r3, at(zs_sem, p), both(cond, far))
-            middle(p, cond)
+                pl.when(more)(lambda: send(way, y, one(p), r1, r3, single_sent, zs_sem + p))
+            middle(p)
+
+        sides(k, hop)
 
     def pair_hop(k):
-        for p, cond, way, far in ways(k):
-            net.recv(V(y, two(p), 0, r1 + rows - r3), at(zp_sem, p), cond)
+        def hop(p, way, more):
+            net.recv(V(y, two(p), 0, ends), zp_sem + p)
             if k < 3:
-                pair(way, p, both(cond, far))
+                pl.when(more)(lambda: pair(way, p))
+
+        sides(k, hop)
 
     def last_hop(k):
-        for p, cond in planes(k):
+        def hop(p, way, more):
             if r3 > r1:
-                net.recv(V(y, one(p), r1, r3), at(m_sem, p), cond)
-            send("y", y, two(p), 0, r2, at(l_sem, p), cond)
-            send("x", every, one(p), r2, rows, at(l_sem, p), cond)
+                net.recv(V(y, one(p), r1, r3), m_sem + p)
+            send("y", y, two(p), 0, r2, last_sent, l_sem + p)
+            send("x", every, one(p), r2, rows, last_sent, l_sem + p)
+
+        sides(k, hop)
 
     def to_core(k):
-        for p, cond in planes(k):
-            net.recv(V(y, two(p), 0, rows), at(l_sem, p), cond)
-            send("c", every, two(p), 0, rows, at(c_sem, p), cond)
+        def hop(p, way, more):
+            net.recv(V(y, two(p), 0, rows), l_sem + p)
+            send("c", every, two(p), 0, rows, core_sent, c_sem)
+
+        sides(k, hop)
 
     def from_core(k):
-        for p, cond in planes(k):
-            net.recv(V(every, two(p), 0, rows, other=True), at(c_sem, p), cond)
+        if k == 3:
+            net.recv(V(every, every, 0, rows, other=True), c_sem)
+
+    def finish():
+        net.wait_sent(V(y, one(z), 0, ends), start_sent)
+        net.wait_sent(V(y, every, 0, rows), last_sent)
+        net.wait_sent(V(every, every, 0, rows), core_sent)
+        if r3 > r1:
+            net.wait_sent(V(y, pl.ds(0, 4), r1, r3), middle_sent)
+
+        def along(count):
+            if r3 > r1:
+                net.wait_sent(V(y, pl.ds(0, count), r1, r3), single_sent)
+            total = 2 * ends * count
+            yy, blocks = min(
+                (yy, n) for yy in (1, 2) for n in range(1, 9) if total % (yy * n * 16) == 0 and total // (yy * n) <= rows
+            )
+            net.wait_sent(V(y if yy == 1 else every, pl.ds(0, blocks), 0, total // (yy * blocks)), pair_sent)
+
+        inner = jnp.logical_and(z > 0, z < 3)
+        pl.when(inner)(lambda: along(5))
+        pl.when(jnp.logical_not(inner))(lambda: along(1))
 
     kinds = (start, first_hop, single_hop, pair_hop, last_hop, to_core, from_core)
-    return [f if i < 2 else functools.partial(f, k) for i, f in enumerate(kinds) for k in range(4)]
-
-
-def at_step(t, groups):
-    for j, group in enumerate(groups):
-        if group:
-
-            def go(group=group):
-                for f in group:
-                    f()
-
-            pl.when(t == j)(go)
+    return [f if i < 2 else functools.partial(f, k) for i, f in enumerate(kinds) for k in range(4)], finish
 
 
 def nn(a, b):
@@ -277,13 +239,12 @@
 def layer_kernel(
     patches, lengths, tasks, master, gain_one, gain_two, qkv_in, out_in, u_in, d_in, cot_hbm,
     out_block, out_patch, out_task, out_stats,
-    GP, GA, GM0, GM1, GM2, LOC, SEL, RES, N1, QKV, PT, CTX, RES2, N2, COT, ACT, GU, MACC, GACC, G2, G2B, DM, DC, LEADR,
-    PAIR, PIN, BOUT, SEND, RECV, ONEHOT, SREC, STSUM, local_sem, send_sem, recv_sem, all_sem,
+    GP, GA, GDS, GUS, LOC, SEL, RES, N1, QKV, PT, CTX, RES2, N2, COT, BACK, ACT, GU, MACC, GACC, G2, G2B, DM, DC, LEADR,
+    PAIR, PIN, BOUT, SEND, RECV, ONEHOT, SREC, STSUM, QIN, OIN, MIN, GIN, own_sem, local_sem, send_sem, recv_sem, all_sem,
 ):
     net = Net(send_sem, recv_sem)
     z, x, y, c, dp, mp = net.z, net.x, net.y, net.c, net.dp, net.mp
     device = dp * 4 + mp
-    GMS = (GM0, GM1, GM2)
 
     barrier = pltpu.get_barrier_semaphore()
     for way, cond in (("x", None), ("y", None), ("c", None), ("u", lambda: z < 3), ("d", lambda: z > 0)):
@@ -299,25 +260,33 @@
 
     cot_copy = pltpu.make_async_copy(cot_hbm.at[pl.ds(mp * IMGS, IMGS)], COT, local_sem.at[0])
     copies = []
-    first = 0
-    for i, (GM, w) in enumerate(zip(GMS, CHUNKS)):
-        for j, weight_in in enumerate((u_in, d_in)):
+    for refs, widths, weight_in in ((GDS, DOWNS, d_in), (GUS, UPS, u_in)):
+        first = 0
+        for ref, w in zip(refs, widths):
             copies.append(
                 pltpu.make_async_copy(
-                    weight_in.at[:, pl.ds(first, w)],
-                    GM.at[j, y, dp, :, own_cols(w)],
-                    local_sem.at[1 + 2 * i + j],
+                    weight_in.at[:, pl.ds(first, w)], ref.at[0, y, dp, :, own_cols(w)], own_sem.at[len(copies)]
                 )
             )
-        first += w
+            first += w
     for copy in copies:
         copy.start()
-    patch_copy = pltpu.make_async_copy(patches, PIN, local_sem.at[7])
+    patch_copy = pltpu.make_async_copy(patches, PIN, local_sem.at[1])
+    small = [
+        pltpu.make_async_copy(src, dst, own_sem.at[len(copies) + i])
+        for i, (src, dst) in enumerate(
+            ((qkv_in, QIN), (out_in, OIN), (master, MIN), (gain_one, GIN.at[0]), (gain_two, GIN.at[1]))
+        )
+    ]
+    for copy in small:
+        copy.start()
     patch_copy.start()
     cot_copy.start()
-
-    qkv = [qkv_in[i].astype(F32) for i in range(3)]
-    outs = out_in[...].astype(F32).T
+    for copy in small:
+        copy.wait()
+
+    qkv = [QIN[i].astype(F32) for i in range(3)]
+    outs = OIN[...].astype(F32).T
     low = lax.broadcasted_iota(jnp.int32, (96, 128), 1) < HEAD_DIM
 
     def tail(v, high):
@@ -332,7 +301,7 @@
         jnp.concatenate(tiles, axis=1).astype(BF16)[None, None]
     )
 
-    LOC[:, 0:PART] = master[...]
+    LOC[:, 0:PART] = MIN[...]
     lane = lax.broadcasted_iota(jnp.int32, (TASKS, PADP - PART), 1)
     LOC[:, PART:PADP] = jnp.where(
         lane == 0, tasks[0, 0].astype(F32), jnp.where(lane == 1, tasks[0, 1].astype(F32), 0.0)
@@ -347,34 +316,22 @@
     run_if(lambda: inner, lambda: pl.semaphore_wait(barrier, 5))
     run_if(lambda: jnp.logical_not(inner), lambda: pl.semaphore_wait(barrier, 4))
 
-    split = (32, 48, 64, 96)
-    gathers = [gather_events(net, GP, half, (16, 16, 16, 16)), gather_events(net, GA, D, split)]
-    gathers += [gather_events(net, GM, w, split) for GM, w in zip(GMS, CHUNKS)]
-    segments = [[gathers[i // 28][i % 28] for i in part] for part in ORDER]
-    position = [0]
-
-    def ahead(n=1):
-        position[0] += n
-        return segments[position[0] - n : position[0]]
-
-    def advance():
-        for f in ahead()[0]:
-            f()
-
-    g1 = gain_one[...].reshape(1, D)
-    g2 = gain_two[...].reshape(1, D)
+    gathers = [gather_events(net, GP, half, (16, 16, 16, 16))]
+    for ref, w, split in zip((GA, *GDS, *GUS), (D, *DOWNS, *UPS), SPLITS):
+        gathers.append(gather_events(net, ref, w, split))
+
+    g1 = GIN[0].reshape(1, D)
+    g2 = GIN[1].reshape(1, D)
     limits = [lengths[b] + LEAD for b in range(IMGS)]
     live = [
         (lax.broadcasted_iota(jnp.int32, (ROWS, 1), 0) < limits[b]).astype(F32) for b in range(IMGS)
     ]
 
-    advance()
-    patch_copy.wait()
-    for b in range(IMGS):
-        RES[b, LEAD:ROWS, :] = PIN[:, b, :].astype(F32)
-    MACC[...] = jnp.zeros_like(MACC)
-    GACC[...] = jnp.zeros_like(GACC)
-    advance()
+    def place_rows():
+        patch_copy.wait()
+        cot_copy.wait()
+        for b in range(IMGS):
+            RES[b, LEAD:ROWS, :] = PIN[:, b, :].astype(F32)
 
     task_rows = lax.broadcasted_iota(jnp.int32, (TASKS, 1), 0)
 
@@ -396,22 +353,23 @@
             ).astype(F32)
         return 0
 
-    lax.fori_loop(0, NDEV, pick, 0)
-    wide = lax.broadcasted_iota(jnp.int32, (4, D), 1)
-    for r in range(25):
-        j, off = (D * r) // PART, (D * r) % PART
-        first = min(D, PART - off)
-        low = SEL[j, 0:4, :]
-        seg = (pltpu.roll(low, PADP - off, 1) if off else low)[:, 0:D]
-        if first < D:
-            seg = jnp.where(wide < first, seg, pltpu.roll(SEL[j + 1, 0:4, :], first, 1)[:, 0:D])
-        for rep in range(2):
-            for b in range(IMGS):
-                RES[b, 25 * rep + r : 25 * rep + r + 1, :] = seg[2 * rep + b : 2 * rep + b + 1]
-
-    advance()
-    for b in range(IMGS):
-        N1[b] = (norm_parts(RES[b])[0] * g1).astype(BF16)
+    def place_prompts():
+        lax.fori_loop(0, NDEV, pick, 0)
+        wide = lax.broadcasted_iota(jnp.int32, (4, D), 1)
+        for r in range(25):
+            j, off = (D * r) // PART, (D * r) % PART
+            first = min(D, PART - off)
+            low = SEL[j, 0:4, :]
+            seg = (pltpu.roll(low, PADP - off, 1) if off else low)[:, 0:D]
+            if first < D:
+                seg = jnp.where(wide < first, seg, pltpu.roll(SEL[j + 1, 0:4, :], first, 1)[:, 0:D])
+            for rep in range(2):
+                for b in range(IMGS):
+                    RES[b, 25 * rep + r : 25 * rep + r + 1, :] = seg[2 * rep + b : 2 * rep + b + 1]
+
+    def norm_one():
+        for b in range(IMGS):
+            N1[b] = (norm_parts(RES[b])[0] * g1).astype(BF16)
 
     def weight(ref, core, first, width, span):
         cols = pl.ds(pl.multiple_of(core * span + first, 128), width)
@@ -422,21 +380,13 @@
     wide = lax.broadcasted_iota(jnp.int32, (1, 640), 1)
     q_scale = jnp.where((wide < 128) | ((wide >= 384) & (wide < 448)), scale, 1.0)
 
-    groups = ahead(2)
-
-    def project(t, _):
-        at_step(t, groups)
-        for core in range(2):
-            w = weight(GA.at[0, t], core, 0, 640, D)
-            mixed = nn(N1[...].reshape(IMGS * ROWS, D), w) * q_scale
-            QKV[2 * t + core] = mixed.astype(BF16).reshape(IMGS, ROWS, 640)
-        return 0
-
-    lax.fori_loop(0, 2, project, 0)
+    def project(m):
+        w = weight(GA.at[0, m // 2], m % 2, 0, 640, D)
+        mixed = nn(N1[...].reshape(IMGS * ROWS, D), w) * q_scale
+        QKV[m] = mixed.astype(BF16).reshape(IMGS, ROWS, 640)
 
     key_rows = lax.broadcasted_iota(jnp.int32, (ROWS, ROWS), 0)
     zero = jnp.zeros((), BF16)
-    groups_a = ahead(ATT)
 
     def attend(t):
         b, m = t // 4, t % 4
@@ -453,26 +403,21 @@
         p1 = soft(k01, keep(left, zero, q01))
         p2 = soft(k2, keep(left, q2v2, zero))
         PT[t, 0], PT[t, 1], PT[t, 2] = p0, p1, p2
-        CTX[b, :, pl.ds(pl.multiple_of(m * 256, 128), 128)] = keep(left, 0.0, tn(p2, q2v2)).astype(BF16)
-        CTX[b, :, pl.ds(pl.multiple_of(m * 256 + 128, 128), 128)] = keep(
+        CTX[b, :, m * 256 : m * 256 + 128] = keep(left, 0.0, tn(p2, q2v2)).astype(BF16)
+        CTX[b, :, m * 256 + 128 : m * 256 + 256] = keep(
             left, tn(p0, v01), tn(p1, v01)
         ).astype(BF16)
 
-    def attend_some(t, _):
-        at_step(t, groups_a)
-        for j in range(8 // ATT):
-            attend(t * (8 // ATT) + j)
-        return 0
-
-    lax.fori_loop(0, ATT, attend_some, 0)
+    def attend_two(t):
+        attend(2 * t)
+        attend(2 * t + 1)
 
     sums = [jnp.zeros((1, 1), F32) for _ in range(3)]
 
     def total(v):
         return jnp.sum(jnp.sum(v, axis=0, keepdims=True), axis=1, keepdims=True)
 
-    for b in range(IMGS):
-        advance()
+    def project_out(b):
         attn = jnp.zeros((ROWS, D), F32)
         for m in range(4):
             attn += nt(CTX[b, :, 256 * m : 256 * m + 256], weight(GA.at[0, m // 2], m % 2, 512, 256, D))
@@ -480,32 +425,58 @@
         res2 = RES[b] + attn
         RES2[b] = res2
         N2[b] = (norm_parts(res2)[0] * g2).astype(BF16)
-    cot_copy.wait()
-
-    def feed(i, yy):
-        GM, w = GMS[i], CHUNKS[i]
-        rows2 = N2[...].reshape(IMGS * ROWS, D)
+
+    def back_units(i, yy):
+        w, first = DOWNS[i], sum(DOWNS[:i])
         cot = COT[...].reshape(IMGS * ROWS, D)
         for core in range(2):
-            up = nn(rows2, weight(GM.at[0, yy], core, 0, w, w))
-            back = nn(cot, weight(GM.at[1, yy], core, 0, w, w))
+            back = nn(cot, weight(GDS[i].at[0, yy], core, 0, w, w))
+            BACK[yy, :, core * D + first : core * D + first + w] = back.astype(BF16)
+
+    def up_units(i, yy):
+        w, first = UPS[i], sum(UPS[:i])
+        rows2 = N2[...].reshape(IMGS * ROWS, D)
+        for core in range(2):
+            up = nn(rows2, weight(GUS[i].at[0, yy], core, 0, w, w))
+            back = BACK[yy, :, core * D + first : core * D + first + w].astype(F32)
             cumul = 0.5 * (1.0 + lax.erf(up * 0.7071067811865476))
             density = jnp.exp(-0.5 * up * up) * 0.3989422804014327
             ACT[:, w * core : w * (core + 1)] = (up * cumul).astype(BF16)
             GU[:, w * core : w * (core + 1)] = (back * (cumul + up * density)).astype(BF16)
-        MACC[...] += nt(ACT[:, 0 : 2 * w], weight(GM.at[1, yy], 0, 0, 2 * w, w)).reshape(IMGS, ROWS, D)
-        GACC[...] += nt(GU[:, 0 : 2 * w], weight(GM.at[0, yy], 0, 0, 2 * w, w)).reshape(IMGS, ROWS, D)
-
-    for i in range(len(CHUNKS)):
-        groups_m = ahead(2)
-
-        def step(t, _, i=i, groups_m=groups_m):
-            at_step(t, groups_m)
-            feed(i, t)
-            return 0
-
-        lax.fori_loop(0, 2, step, 0)
-    advance()
+
+    def add_units(i, yy):
+        w, first = UPS[i], sum(UPS[:i])
+        d = max(d for d in range(len(DOWNS)) if sum(DOWNS[:d]) <= first)
+        inside = first - sum(DOWNS[:d])
+        if w == DOWNS[d]:
+            mlp = nt(ACT[:, 0 : 2 * w], weight(GDS[d].at[0, yy], 0, 0, 2 * w, w))
+        else:
+            mlp = sum(
+                nt(ACT[:, w * core : w * (core + 1)], weight(GDS[d].at[0, yy], core, inside, w, DOWNS[d]))
+                for core in range(2)
+            )
+        grad = nt(GU[:, 0 : 2 * w], weight(GUS[i].at[0, yy], 0, 0, 2 * w, w))
+        mlp, grad = mlp.reshape(IMGS, ROWS, D), grad.reshape(IMGS, ROWS, D)
+        if i == 0 and yy == 0:
+            MACC[...] = mlp
+            GACC[...] = grad
+        else:
+            MACC[...] += mlp
+            GACC[...] += grad
+
+    steps = [place_rows, place_prompts, norm_one]
+    steps += [functools.partial(project, m) for m in range(4)]
+    steps += [functools.partial(attend_two, t) for t in range(4)]
+    steps += [functools.partial(project_out, b) for b in range(IMGS)]
+    steps += [functools.partial(back_units, i, yy) for i in range(len(DOWNS)) for yy in range(2)]
+    for i in range(len(UPS)):
+        for yy in range(2):
+            steps += [functools.partial(up_units, i, yy), functools.partial(add_units, i, yy)]
+    for item in ORDER:
+        if item < 1000:
+            gathers[item // 28][0][item % 28]()
+        else:
+            steps[item - 1000]()
 
     for b in range(IMGS):
         g = COT[b].astype(F32) + norm_back(RES2[b], g2, GACC[b])
@@ -610,7 +581,7 @@
         BOUT[b] = block.astype(BF16)
         sums[0] += total(block * block * live[b])
         sums[2] += total(mlp * mlp * live[b])
-    block_copy = pltpu.make_async_copy(BOUT, out_block, local_sem.at[8])
+    block_copy = pltpu.make_async_copy(BOUT, out_block, local_sem.at[2])
     block_copy.start()
 
     def add_image(b, acc):
@@ -640,11 +611,12 @@
     for b in range(IMGS):
         PAIR[:, b : b + 1, :] = GACC[b, LEAD:ROWS, :][:, None, :]
     PIN[...] = PAIR[...].astype(BF16)
-    patch_out = pltpu.make_async_copy(PIN, out_patch, local_sem.at[9])
+    patch_out = pltpu.make_async_copy(PIN, out_patch, local_sem.at[3])
     patch_out.start()
     for b in range(IMGS):
         wait_all(RECV.at[b], 2 * b)
-    net.finish()
+    for gather in gathers:
+        gather[1]()
     block_copy.wait()
     wait_all(SREC, 5)
     out_stats[...] = jnp.sum(SREC[...], axis=0)
@@ -654,20 +626,13 @@
 
 def update_kernel(
     task_grad, stats, master, first_moment, second_moment, block_in, patch_in,
-    out_grad, out_first, out_second, out_master, out_copy, out_norm, out_rms, block_out, patch_out,
-    block_held, patch_held, sem,
+    out_grad, out_first, out_second, out_master, out_copy, out_norm, out_rms, block_out, patch_out, sem,
 ):
-    inward = [
-        pltpu.make_async_copy(block_in.at[0], block_held.at[0], sem.at[0]),
-        pltpu.make_async_copy(block_in.at[1], block_held.at[1], sem.at[1]),
-        pltpu.make_async_copy(patch_in, patch_held, sem.at[2]),
+    copies = [
+        pltpu.make_async_copy(block_in, block_out, sem.at[0]),
+        pltpu.make_async_copy(patch_in, patch_out, sem.at[1]),
     ]
-    outward = [
-        pltpu.make_async_copy(block_held.at[0], block_out.at[0], sem.at[3]),
-        pltpu.make_async_copy(block_held.at[1], block_out.at[1], sem.at[4]),
-        pltpu.make_async_copy(patch_held, patch_out, sem.at[5]),
-    ]
-    for copy in inward:
+    for copy in copies:
         copy.start()
     st = stats[0:1, :]
     norm = jnp.sqrt(st[0:1, 0:1])
@@ -688,10 +653,7 @@
     rms = jnp.sqrt(st / (st[0:1, 4:5] * D))
     for i in range(3):
         out_rms[i] = rms[0, i + 1]
-    for copy, after in zip(inward, outward):
-        copy.wait()
-        after.start()
-    for copy in outward:
+    for copy in copies:
         copy.wait()
 
 
@@ -711,14 +673,13 @@
             jax.ShapeDtypeStruct((TASKS, PART), F32),
             jax.ShapeDtypeStruct((1, 128), F32),
         ],
-        in_specs=[anywhere, smem, smem, vmem, vmem, vmem, vmem, vmem, anywhere, anywhere, anywhere],
+        in_specs=[anywhere, smem, smem] + [anywhere] * 8,
         out_specs=[anywhere] * 2 + [vmem] * 2,
         scratch_shapes=[
             V((1, 2, 8, 16, PADP), BF16),
             V((1, 2, 8, 96, 2 * D), BF16),
-            V((2, 2, 8, 96, 2 * CHUNKS[0]), BF16),
-            V((2, 2, 8, 96, 2 * CHUNKS[1]), BF16),
-            V((2, 2, 8, 96, 2 * CHUNKS[2]), BF16),
+            [V((1, 2, 8, 96, 2 * w), BF16) for w in DOWNS],
+            [V((1, 2, 8, 96, 2 * w), BF16) for w in UPS],
             V((TASKS, PADP), F32),
             V((16, 4, PADP), F32),
             V((IMGS, ROWS, D), F32),
@@ -729,8 +690,9 @@
             V((IMGS, ROWS, D), F32),
             V((IMGS, ROWS, D), BF16),
             V((IMGS, ROWS, D), BF16),
-            V((IMGS * ROWS, 2 * CHUNKS[0]), BF16),
-            V((IMGS * ROWS, 2 * CHUNKS[0]), BF16),
+            V((2, IMGS * ROWS, 2 * D), BF16),
+            V((IMGS * ROWS, 2 * max(UPS)), BF16),
+            V((IMGS * ROWS, 2 * max(UPS)), BF16),
             V((IMGS, ROWS, D), F32),
             V((IMGS, ROWS, D), F32),
             V((IMGS, ROWS, D), F32),
@@ -746,9 +708,14 @@
             V((NDEV, IMGS, TASKS, 128), F32),
             V((NDEV, 1, 128), F32),
             V((1, 128), F32),
-            pltpu.SemaphoreType.DMA((10,)),
-            pltpu.SemaphoreType.DMA((RING,)),
-            pltpu.SemaphoreType.DMA((13 + 21 * (1 + len(CHUNKS)),)),
+            V((3, 96, 192), BF16),
+            V((192, 96), BF16),
+            V((TASKS, PART), F32),
+            V((2, D), F32),
+            pltpu.SemaphoreType.DMA((5 + len(DOWNS) + len(UPS),)),
+            pltpu.SemaphoreType.DMA((4,)),
+            pltpu.SemaphoreType.DMA((6 * (2 + len(DOWNS) + len(UPS)),)),
+            pltpu.SemaphoreType.DMA((10 + 18 * (1 + len(DOWNS) + len(UPS)),)),
             pltpu.SemaphoreType.DMA((6,)),
         ],
         compiler_params=pltpu.CompilerParams(
@@ -769,9 +736,9 @@
             jax.ShapeDtypeStruct((IMGS, ROWS, D), BF16),
             jax.ShapeDtypeStruct((PATCH, IMGS, D), BF16),
         ],
-        in_specs=[vmem] * 5 + [anywhere] * 2,
+        in_specs=[vmem] * 7,
         out_specs=[vmem] * 5 + [smem] * 2 + [anywhere] * 2,
-        scratch_shapes=[V((IMGS, ROWS, D), BF16), V((PATCH, IMGS, D), BF16), pltpu.SemaphoreType.DMA((6,))],
+        scratch_shapes=[pltpu.SemaphoreType.DMA((2,))],
     )(task, stats, prompt_master, first_moment, second_moment, block, patch)
     return (
         block_out, patch_out.transpose(1, 0, 2), grad, norm.reshape(()), first, second, master, copy, rms,

time: 96.1 us -> 93.2 us (0.970)
  Pallas kernels: 95.1 us -> 92.2 us
    pallas_call x1, Pallas kernels: 91.4 us -> 89 us  [fast_body(): pl.pallas_call(layer_kernel, out_shape=[jax.ShapeDtypeStruct((IMGS, ROWS,...]
where the time goes in v3:
time: 93.2 us; the launch traced here: 93 us
  Pallas kernels  92.2 us (99%)
    pallas_call x1, Pallas kernels, fast_body(): pl.pallas_call(layer_kernel, out_shape=[jax.ShapeDtypeStruct((IMGS, ROWS,...  89 us
    pallas_call x1, Pallas kernels, fast_body(): pl.pallas_call(update_kernel, out_shape=[state] * 4 + [jax.ShapeDtypeStru...  3.17 us

profile of v3, /device:TPU:0, one launch (start us, length us, event | category | flops | bytes accessed | tf_op | source)
XLA Modules:
  0.0 93.0 jit_solution(13567669682514756336)
XLA Ops:
  0.6 89.0 %shard_map.196 = (bf16[2,256,768]{2,1,0:T(8,128)(2,1)}, bf16[206,2,768]{2,1,0:T(2,128)(2,1)}, f32[8,1200]{1,0:T(8,128)}, f32[1,128]{1,0:T(1,128)}) custom-call(bf16[206,2,768]{2,1,0:T(2,128)(2,1)} %bitcast.6, s32[2]{0:T(128)} %lengths.1, s32[1,2]{1,0:T(1,128)} %bitcast.9, f32[8,1200]{1,0:T(8,128)} %master.3, f32[768]{0:T(1024)} %gain_one.1, f32[768]{0:T(1024)} %gain_two.1, ...), custom_call_target="tpu_custom_call" | custom-call | tf_op jit(solution)/shard_map/pallas_call | solution.py:668
  89.7 3.2 %shard_map.197 = (f32[8,1200]{1,0:T(8,128)}, f32[8,1200]{1,0:T(8,128)}, f32[8,1200]{1,0:T(8,128)}, f32[8,1200]{1,0:T(8,128)}, bf16[8,1200]{1,0:T(8,128)(2,1)}, /...) custom-call(f32[8,1200]{1,0:T(8,128)} %get-tuple-element.22.task_grad, ...), custom_call_target="tpu_custom_call" | custom-call | tf_op jit(solution)/shard_map/pallas_call | solution.py:729

commit v4 on v3

--- a/solution.py
+++ b/solution.py
@@ -33,15 +33,15 @@
 NDEV = 32
 DOWNS = (384, 384)
 UPS = (384, 384)
-SPLITS = ((16, 48, 64, 96), (32, 48, 80, 96), (16, 48, 64, 96), (32, 48, 80, 96), (16, 48, 64, 96))
+SPLITS = ((16, 48, 80, 96), (32, 32, 64, 96), (16, 48, 64, 96), (32, 48, 48, 96), (32, 48, 80, 96))
 ORDER = (
-    0, 28, 56, 84, 1000, 4, 16, 32, 37, 60, 44, 13, 17, 72, 41, 112, 38, 45, 20, 14,
-    18, 65, 48, 42, 46, 15, 19, 39, 69, 49, 140, 66, 21, 76, 121, 73, 116, 22, 43, 47,
-    23, 93, 70, 128, 88, 27, 50, 1001, 149, 67, 100, 122, 51, 1002, 125, 74, 71, 75, 55, 144,
-    1003, 97, 156, 1004, 94, 1005, 123, 150, 126, 129, 130, 1006, 1007, 153, 98, 101, 1008, 95, 151, 78,
-    77, 1009, 127, 79, 131, 1010, 157, 132, 133, 134, 154, 102, 83, 1011, 1013, 99, 103, 1014, 135, 160,
-    104, 1012, 158, 139, 1017, 155, 105, 161, 159, 1018, 106, 1019, 107, 162, 1020, 163, 111, 1015, 1016, 167,
-    1021, 1022, 1023, 1024,
+    0, 28, 112, 84, 56, 4, 16, 32, 37, 1000, 44, 13, 121, 41, 45, 38, 14, 17, 18, 60,
+    20, 72, 42, 48, 122, 49, 65, 39, 15, 19, 93, 116, 21, 46, 69, 22, 23, 43, 140, 47,
+    66, 88, 128, 76, 27, 1001, 94, 100, 125, 73, 50, 123, 1002, 70, 51, 74, 129, 149, 132, 55,
+    1003, 67, 97, 1004, 1005, 144, 156, 104, 1006, 126, 71, 77, 75, 1007, 78, 98, 130, 1008, 102, 150,
+    153, 1009, 79, 95, 133, 160, 127, 131, 101, 1010, 134, 83, 1011, 151, 1013, 99, 103, 154, 157, 135,
+    1012, 158, 1014, 1017, 105, 139, 106, 1018, 107, 155, 159, 1019, 161, 1020, 111, 162, 1015, 163, 1016, 1021,
+    167, 1022, 1023, 1024,
 )
 
 
@@ -222,8 +222,7 @@
     return shifted * scaled, scaled
 
 
-def norm_back(v, gain, upstream):
-    normal, scaled = norm_parts(v)
+def norm_back(normal, scaled, gain, upstream):
     weighted = upstream * gain
     return scaled * (
         weighted
@@ -239,8 +238,8 @@
 def layer_kernel(
     patches, lengths, tasks, master, gain_one, gain_two, qkv_in, out_in, u_in, d_in, cot_hbm,
     out_block, out_patch, out_task, out_stats,
-    GP, GA, GDS, GUS, LOC, SEL, RES, N1, QKV, PT, CTX, RES2, N2, COT, BACK, ACT, GU, MACC, GACC, G2, G2B, DM, DC, LEADR,
-    PAIR, PIN, BOUT, SEND, RECV, ONEHOT, SREC, STSUM, QIN, OIN, MIN, GIN, own_sem, local_sem, send_sem, recv_sem, all_sem,
+    GP, GA, GDS, GUS, LOC, SEL, RES, N1, QKV, PT, CTX, RES2, N2, NRM1, NRM2, SC1, SC2, COT, BACK, ACT, GU, MACC, GACC, G2, G2B, DM, DC, LEADR,
+    PAIR, PIN, SEND, RECV, ONEHOT, SREC, STSUM, QIN, OIN, MIN, GIN, own_sem, local_sem, send_sem, recv_sem, all_sem,
 ):
     net = Net(send_sem, recv_sem)
     z, x, y, c, dp, mp = net.z, net.x, net.y, net.c, net.dp, net.mp
@@ -369,7 +368,9 @@
 
     def norm_one():
         for b in range(IMGS):
-            N1[b] = (norm_parts(RES[b])[0] * g1).astype(BF16)
+            normal, SC1[b] = norm_parts(RES[b])
+            NRM1[b] = normal
+            N1[b] = (normal * g1).astype(BF16)
 
     def weight(ref, core, first, width, span):
         cols = pl.ds(pl.multiple_of(core * span + first, 128), width)
@@ -424,7 +425,9 @@
         sums[1] += total(attn * attn * live[b])
         res2 = RES[b] + attn
         RES2[b] = res2
-        N2[b] = (norm_parts(res2)[0] * g2).astype(BF16)
+        normal, SC2[b] = norm_parts(res2)
+        NRM2[b] = normal
+        N2[b] = (normal * g2).astype(BF16)
 
     def back_units(i, yy):
         w, first = DOWNS[i], sum(DOWNS[:i])
@@ -433,29 +436,30 @@
             back = nn(cot, weight(GDS[i].at[0, yy], core, 0, w, w))
             BACK[yy, :, core * D + first : core * D + first + w] = back.astype(BF16)
 
-    def up_units(i, yy):
+    def up_units(i, core):
         w, first = UPS[i], sum(UPS[:i])
         rows2 = N2[...].reshape(IMGS * ROWS, D)
-        for core in range(2):
+        here = pl.ds(pl.multiple_of(core * w, 128), w)
+        for yy in range(2):
             up = nn(rows2, weight(GUS[i].at[0, yy], core, 0, w, w))
-            back = BACK[yy, :, core * D + first : core * D + first + w].astype(F32)
+            back = BACK[yy, :, pl.ds(pl.multiple_of(core * D + first, 128), w)].astype(F32)
             cumul = 0.5 * (1.0 + lax.erf(up * 0.7071067811865476))
             density = jnp.exp(-0.5 * up * up) * 0.3989422804014327
-            ACT[:, w * core : w * (core + 1)] = (up * cumul).astype(BF16)
-            GU[:, w * core : w * (core + 1)] = (back * (cumul + up * density)).astype(BF16)
+            ACT[yy, :, here] = (up * cumul).astype(BF16)
+            GU[yy, :, here] = (back * (cumul + up * density)).astype(BF16)
 
     def add_units(i, yy):
         w, first = UPS[i], sum(UPS[:i])
         d = max(d for d in range(len(DOWNS)) if sum(DOWNS[:d]) <= first)
         inside = first - sum(DOWNS[:d])
         if w == DOWNS[d]:
-            mlp = nt(ACT[:, 0 : 2 * w], weight(GDS[d].at[0, yy], 0, 0, 2 * w, w))
+            mlp = nt(ACT[yy, :, 0 : 2 * w], weight(GDS[d].at[0, yy], 0, 0, 2 * w, w))
         else:
             mlp = sum(
-                nt(ACT[:, w * core : w * (core + 1)], weight(GDS[d].at[0, yy], core, inside, w, DOWNS[d]))
+                nt(ACT[yy, :, w * core : w * (core + 1)], weight(GDS[d].at[0, yy], core, inside, w, DOWNS[d]))
                 for core in range(2)
             )
-        grad = nt(GU[:, 0 : 2 * w], weight(GUS[i].at[0, yy], 0, 0, 2 * w, w))
+        grad = nt(GU[yy, :, 0 : 2 * w], weight(GUS[i].at[0, yy], 0, 0, 2 * w, w))
         mlp, grad = mlp.reshape(IMGS, ROWS, D), grad.reshape(IMGS, ROWS, D)
         if i == 0 and yy == 0:
             MACC[...] = mlp
@@ -470,8 +474,8 @@
     steps += [functools.partial(project_out, b) for b in range(IMGS)]
     steps += [functools.partial(back_units, i, yy) for i in range(len(DOWNS)) for yy in range(2)]
     for i in range(len(UPS)):
-        for yy in range(2):
-            steps += [functools.partial(up_units, i, yy), functools.partial(add_units, i, yy)]
+        steps += [functools.partial(up_units, i, c), functools.partial(up_units, i, 1 - c)]
+        steps += [functools.partial(add_units, i, yy) for yy in range(2)]
     for item in ORDER:
         if item < 1000:
             gathers[item // 28][0][item % 28]()
@@ -479,7 +483,7 @@
             steps[item - 1000]()
 
     for b in range(IMGS):
-        g = COT[b].astype(F32) + norm_back(RES2[b], g2, GACC[b])
+        g = COT[b].astype(F32) + norm_back(NRM2[b], SC2[b], g2, GACC[b])
         G2[b] = g
         G2B[b] = g.astype(BF16)
 
@@ -519,28 +523,34 @@
             DM[m, b, :, 384:512] = keep(left, tn(s2, k2) * scale, nn(p2, c2)).astype(BF16)
             DM[m, b, :, 512:640] = keep(left, nn(s2, q2v2), 0.0).astype(BF16)
 
-    def grad_rows(b, first, last):
-        grad = jnp.zeros((last - first, D), F32)
+    def grad_rows(rows, first, last):
+        count = last - first
+        grad = jnp.zeros((len(rows) * count, D), F32)
         for m in range(4):
-            grad += nt(DM[m, b, first:last], weight(GA.at[0, m // 2], m % 2, 0, 640, D))
-        GACC[b, first:last] = G2[b, first:last] + norm_back(RES[b, first:last], g1, grad)
+            mixed = jnp.concatenate([DM[m, b, first:last] for b in rows], axis=0)
+            grad += nt(mixed, weight(GA.at[0, m // 2], m % 2, 0, 640, D))
+        for i, b in enumerate(rows):
+            part = grad[count * i : count * (i + 1)]
+            GACC[b, first:last] = G2[b, first:last] + norm_back(NRM1[b, first:last], SC1[b, first:last], g1, part)
 
     def swap(k, src, dst, sems):
-        other = lax.rem(device + k, NDEV)
+        to_dp, to_mp = (dp + k // 4) & 7, (mp + k) & 3
+        other = to_dp * 4 + to_mp
         pltpu.make_async_remote_copy(
             src_ref=src(other),
             dst_ref=dst,
             send_sem=all_sem.at[sems],
             recv_sem=all_sem.at[sems + 1],
-            device_id=(other // 4, lax.rem(other, 4)),
+            device_id=(to_dp, to_mp),
             device_id_type=MESH,
         ).start()
 
-    wide = lax.broadcasted_iota(jnp.int32, (2, PADP), 1)
-
-    def to_owners(b):
+    wide = lax.broadcasted_iota(jnp.int32, (4, PADP), 1)
+
+    def to_owners():
         for rep in range(2):
-            LEADR[:, rep : rep + 1, :] = GACC[b, 25 * rep : 25 * rep + 25, :][:, None, :]
+            for b in range(IMGS):
+                LEADR[:, 2 * rep + b : 2 * rep + b + 1, :] = GACC[b, 25 * rep : 25 * rep + 25, :][:, None, :]
         for q in range(16):
             r, off = (PART * q) // D, (PART * q) % D
             msg, have = None, -off
@@ -553,12 +563,13 @@
                 r += 1
             msg = jnp.where(wide < PART, msg, 0.0).astype(BF16)
             for rep in range(2):
-                SEND[b, 16 * rep + q] = jnp.concatenate(
-                    [msg[rep : rep + 1, 0:half], msg[rep : rep + 1, half:PADP]], axis=0
+                SEND[16 * rep + q] = jnp.concatenate(
+                    [msg[2 * rep + b : 2 * rep + b + 1, half * h : half * h + half] for b in range(IMGS) for h in range(2)],
+                    axis=0,
                 )
         for k in range(1, NDEV):
-            swap(k, lambda other: SEND.at[b, other], RECV.at[b, device], 2 * b)
-        RECV[b, pl.ds(device, 1)] = SEND[b, pl.ds(device, 1)]
+            swap(k, lambda other: SEND.at[other], RECV.at[device], 0)
+        RECV[pl.ds(device, 1)] = SEND[pl.ds(device, 1)]
 
     def others(ref):
         return ref.at[pl.ds(0, NDEV - 1)]
@@ -566,36 +577,32 @@
     def wait_all(ref, sem):
         pltpu.make_async_copy(others(ref), others(ref), all_sem.at[sem]).wait()
 
-    attend_back(0)
-    grad_rows(0, 0, ROWS)
-    to_owners(0)
-    attend_back(1)
     some = 64
-    grad_rows(1, 0, some)
-    to_owners(1)
-
-    grad_rows(1, some, ROWS)
+    for b in range(IMGS):
+        attend_back(b)
+    grad_rows((0, 1), 0, some)
+    to_owners()
+
+    grad_rows((0, 1), some, ROWS)
     for b in range(IMGS):
         mlp = MACC[b]
         block = RES2[b] + mlp
-        BOUT[b] = block.astype(BF16)
+        out_block[b] = block.astype(BF16)
         sums[0] += total(block * block * live[b])
         sums[2] += total(mlp * mlp * live[b])
-    block_copy = pltpu.make_async_copy(BOUT, out_block, local_sem.at[2])
-    block_copy.start()
-
-    def add_image(b, acc):
-        wait_all(RECV.at[b], 2 * b + 1)
-
-        def add(s, acc):
-            rows = RECV[b, s].astype(F32)
+
+    wait_all(RECV, 1)
+
+    def add(s, acc):
+        rows = RECV[s].astype(F32)
+        low, high = acc
+        for b in range(IMGS):
             hot = jnp.concatenate([ONEHOT[s, b]] * (half // 128), axis=1)
-            return acc[0] + hot * rows[0:1], acc[1] + hot * rows[1:2]
-
-        return lax.fori_loop(0, NDEV, add, acc, unroll=8)
+            low, high = low + hot * rows[2 * b : 2 * b + 1], high + hot * rows[2 * b + 1 : 2 * b + 2]
+        return low, high
 
     acc = (jnp.zeros((TASKS, half), F32), jnp.zeros((TASKS, half), F32))
-    acc = add_image(1, add_image(0, acc))
+    acc = lax.fori_loop(0, NDEV, add, acc, unroll=8)
     square = total(acc[0] * acc[0]) + total(acc[1] * acc[1])
     lane = lax.broadcasted_iota(jnp.int32, (1, 128), 1)
     count = (limits[0] + limits[1]).astype(F32)
@@ -605,23 +612,18 @@
     STSUM[...] = stats
     SREC[pl.ds(device, 1)] = stats[None]
     for k in range(1, NDEV):
-        swap(k, lambda other: STSUM, SREC.at[device], 4)
+        swap(k, lambda other: STSUM, SREC.at[device], 2)
 
     out_task[...] = jnp.concatenate(acc, axis=1)[:, 0:PART]
     for b in range(IMGS):
         PAIR[:, b : b + 1, :] = GACC[b, LEAD:ROWS, :][:, None, :]
-    PIN[...] = PAIR[...].astype(BF16)
-    patch_out = pltpu.make_async_copy(PIN, out_patch, local_sem.at[3])
-    patch_out.start()
-    for b in range(IMGS):
-        wait_all(RECV.at[b], 2 * b)
+    out_patch[...] = PAIR[...].astype(BF16)
+    wait_all(RECV, 0)
     for gather in gathers:
         gather[1]()
-    block_copy.wait()
-    wait_all(SREC, 5)
+    wait_all(SREC, 3)
     out_stats[...] = jnp.sum(SREC[...], axis=0)
-    wait_all(SREC, 4)
-    patch_out.wait()
+    wait_all(SREC, 2)
 
 
 def update_kernel(
@@ -668,13 +670,13 @@
     block, patch, task, stats = pl.pallas_call(
         layer_kernel,
         out_shape=[
-            jax.ShapeDtypeStruct((IMGS, ROWS, D), BF16),
-            jax.ShapeDtypeStruct((PATCH, IMGS, D), BF16),
-            jax.ShapeDtypeStruct((TASKS, PART), F32),
-            jax.ShapeDtypeStruct((1, 128), F32),
+            V((IMGS, ROWS, D), BF16),
+            V((PATCH, IMGS, D), BF16),
+            V((TASKS, PART), F32),
+            V((1, 128), F32),
         ],
         in_specs=[anywhere, smem, smem] + [anywhere] * 8,
-        out_specs=[anywhere] * 2 + [vmem] * 2,
+        out_specs=[vmem] * 4,
         scratch_shapes=[
             V((1, 2, 8, 16, PADP), BF16),
             V((1, 2, 8, 96, 2 * D), BF16),
@@ -689,22 +691,25 @@
             V((IMGS, ROWS, 1024), BF16),
             V((IMGS, ROWS, D), F32),
             V((IMGS, ROWS, D), BF16),
+            V((IMGS, ROWS, D), F32),
+            V((IMGS, ROWS, D), F32),
+            V((IMGS, ROWS, 1), F32),
+            V((IMGS, ROWS, 1), F32),
             V((IMGS, ROWS, D), BF16),
             V((2, IMGS * ROWS, 2 * D), BF16),
-            V((IMGS * ROWS, 2 * max(UPS)), BF16),
-            V((IMGS * ROWS, 2 * max(UPS)), BF16),
+            V((2, IMGS * ROWS, 2 * max(UPS)), BF16),
+            V((2, IMGS * ROWS, 2 * max(UPS)), BF16),
             V((IMGS, ROWS, D), F32),
             V((IMGS, ROWS, D), F32),
             V((IMGS, ROWS, D), F32),
             V((IMGS, ROWS, D), BF16),
             V((4, IMGS, ROWS, 640), BF16),
             V((4, IMGS, ROWS, 256), BF16),
-            V((25, 2, D), F32),
+            V((25, 4, D), F32),
             V((PATCH, IMGS, D), F32),
             V((PATCH, IMGS, D), BF16),
-            V((IMGS, ROWS, D), BF16),
-            V((IMGS, NDEV, 2, PADP // 2), BF16),
-            V((IMGS, NDEV, 2, PADP // 2), BF16),
+            V((NDEV, 2 * IMGS, PADP // 2), BF16),
+            V((NDEV, 2 * IMGS, PADP // 2), BF16),
             V((NDEV, IMGS, TASKS, 128), F32),
             V((NDEV, 1, 128), F32),
             V((1, 128), F32),
@@ -713,10 +718,10 @@
             V((TASKS, PART), F32),
             V((2, D), F32),
             pltpu.SemaphoreType.DMA((5 + len(DOWNS) + len(UPS),)),
-            pltpu.SemaphoreType.DMA((4,)),
+            pltpu.SemaphoreType.DMA((2,)),
             pltpu.SemaphoreType.DMA((6 * (2 + len(DOWNS) + len(UPS)),)),
             pltpu.SemaphoreType.DMA((10 + 18 * (1 + len(DOWNS) + len(UPS)),)),
-            pltpu.SemaphoreType.DMA((6,)),
+            pltpu.SemaphoreType.DMA((4,)),
         ],
         compiler_params=pltpu.CompilerParams(
             collective_id=0, has_side_effects=True, vmem_limit_bytes=58 << 20
@@ -726,6 +731,10 @@
         w_qkv.transpose(1, 0, 2), w_out, w_up, w_down.T, cotangent,
     )
     state = jax.ShapeDtypeStruct((TASKS, PART), F32)
+
+    def keep_near(v):
+        return pltpu.with_memory_space_constraint(v, pltpu.VMEM)
+
     grad, first, second, master, copy, norm, rms, block_out, patch_out = pl.pallas_call(
         update_kernel,
         out_shape=[state] * 4
@@ -739,7 +748,9 @@
         in_specs=[vmem] * 7,
         out_specs=[vmem] * 5 + [smem] * 2 + [anywhere] * 2,
         scratch_shapes=[pltpu.SemaphoreType.DMA((2,))],
-    )(task, stats, prompt_master, first_moment, second_moment, block, patch)
+    )(
+        keep_near(task), keep_near(stats), prompt_master, first_moment, second_moment, keep_near(block), keep_near(patch),
+    )
     return (
         block_out, patch_out.transpose(1, 0, 2), grad, norm.reshape(()), first, second, master, copy, rms,
     )

time: 93.2 us -> 91 us (0.976)
  Pallas kernels: 92.2 us -> 89.9 us
    pallas_call x1, Pallas kernels: 89 us -> 87.3 us  [fast_body(): pl.pallas_call(layer_kernel, out_shape=[V((IMGS, ROWS, D), BF16), V((PATC...]
where the time goes in v4:
time: 91 us; the launch traced here: 90.8 us
  Pallas kernels  89.9 us (99%)
    pallas_call x1, Pallas kernels, fast_body(): pl.pallas_call(layer_kernel, out_shape=[V((IMGS, ROWS, D), BF16), V((PATC...  87.3 us
    pallas_call x1, Pallas kernels, fast_body(): pl.pallas_call(update_kernel, out_shape=[state] * 4 + [jax.ShapeDtypeStru...  2.6 us

profile of v4, /device:TPU:0, one launch (start us, length us, event | category | flops | bytes accessed | tf_op | source)
XLA Modules:
  0.0 90.8 jit_solution(17507817201731409788)
XLA Ops:
  0.6 87.3 %shard_map.196 = (bf16[2,256,768]{2,1,0:T(8,128)(2,1)S(1)}, bf16[206,2,768]{2,1,0:T(2,128)(2,1)S(1)}, f32[8,1200]{1,0:T(8,128)S(1)}, f32[1,128]{1,0:T(1,128)S(1)}) custom-call(bf16[206,2,768]{2,1,0:T(2,128)(2,1)} %bitcast.6, s32[2]{0:T(128)} %lengths.1, s32[1,2]{1,0:T(1,128)} %bitcast.9, f32[8,1200]{1,0:T(8,128)} %master.3, f32[768]{0:T(1024)} %gain_one.1, ...), custom_call_target="tpu_custom_call" | custom-call | tf_op jit(solution)/shard_map/pallas_call | solution.py:670
  88.0 2.6 %shard_map.197 = (f32[8,1200]{1,0:T(8,128)}, f32[8,1200]{1,0:T(8,128)}, f32[8,1200]{1,0:T(8,128)}, f32[8,1200]{1,0:T(8,128)}, bf16[8,1200]{1,0:T(8,128)(2,1)}, /...) custom-call(f32[8,1200]{1,0:T(8,128)S(1)} %get-tuple-element.22.task_grad, ...), custom_call_target="tpu_custom_call" | custom-call | tf_op jit(solution)/shard_map/pallas_call | solution.py:738

commit v5 on v4

--- a/solution.py
+++ b/solution.py
@@ -31,16 +31,16 @@
 PART = 1200
 PADP = 1280
 NDEV = 32
-DOWNS = (384, 384)
-UPS = (384, 384)
-SPLITS = ((16, 48, 80, 96), (32, 32, 64, 96), (16, 48, 64, 96), (32, 48, 48, 96), (32, 48, 80, 96))
+DOWNS = (512, 256)
+UPS = (512, 256)
+SPLITS = ((16, 48, 80, 96), (32, 48, 64, 96), (16, 48, 48, 96), (32, 48, 64, 96), (16, 32, 64, 96))
 ORDER = (
-    0, 28, 112, 84, 56, 4, 16, 32, 37, 1000, 44, 13, 121, 41, 45, 38, 14, 17, 18, 60,
-    20, 72, 42, 48, 122, 49, 65, 39, 15, 19, 93, 116, 21, 46, 69, 22, 23, 43, 140, 47,
-    66, 88, 128, 76, 27, 1001, 94, 100, 125, 73, 50, 123, 1002, 70, 51, 74, 129, 149, 132, 55,
-    1003, 67, 97, 1004, 1005, 144, 156, 104, 1006, 126, 71, 77, 75, 1007, 78, 98, 130, 1008, 102, 150,
-    153, 1009, 79, 95, 133, 160, 127, 131, 101, 1010, 134, 83, 1011, 151, 1013, 99, 103, 154, 157, 135,
-    1012, 158, 1014, 1017, 105, 139, 106, 1018, 107, 155, 159, 1019, 161, 1020, 111, 162, 1015, 163, 1016, 1021,
+    28, 56, 0, 1000, 112, 32, 84, 44, 4, 16, 37, 140, 13, 41, 17, 38, 14, 18, 48, 60,
+    45, 42, 144, 121, 65, 21, 22, 39, 15, 19, 46, 156, 20, 23, 43, 47, 69, 72, 116, 149,
+    49, 27, 1001, 93, 66, 50, 1002, 51, 128, 70, 160, 73, 125, 122, 76, 88, 150, 74, 55, 1003,
+    1004, 1005, 67, 129, 1006, 94, 1007, 126, 71, 153, 132, 77, 123, 75, 1008, 78, 130, 1009, 97, 157,
+    1010, 79, 127, 131, 1011, 1012, 95, 133, 154, 100, 151, 158, 83, 98, 102, 101, 1013, 134, 1014, 135,
+    161, 1017, 99, 155, 104, 103, 159, 139, 1018, 162, 106, 1019, 105, 107, 1020, 111, 163, 1015, 1016, 1021,
     167, 1022, 1023, 1024,
 )
 
@@ -236,10 +236,10 @@
 
 
 def layer_kernel(
-    patches, lengths, tasks, master, gain_one, gain_two, qkv_in, out_in, u_in, d_in, cot_hbm,
-    out_block, out_patch, out_task, out_stats,
+    patches, lengths_in, tasks_in, master, first_moment, second_moment, gain_one, gain_two, qkv_in, out_in, u_in, d_in,
+    cot_hbm, out_block, out_patch, out_task, out_stats, MIN, FIRST, SECOND,
     GP, GA, GDS, GUS, LOC, SEL, RES, N1, QKV, PT, CTX, RES2, N2, NRM1, NRM2, SC1, SC2, COT, BACK, ACT, GU, MACC, GACC, G2, G2B, DM, DC, LEADR,
-    PAIR, PIN, SEND, RECV, ONEHOT, SREC, STSUM, QIN, OIN, MIN, GIN, own_sem, local_sem, send_sem, recv_sem, all_sem,
+    PAIR, PIN, SEND, RECV, ONEHOT, SREC, STSUM, QIN, OIN, GIN, lengths, tasks, own_sem, local_sem, send_sem, recv_sem, all_sem,
 ):
     net = Net(send_sem, recv_sem)
     z, x, y, c, dp, mp = net.z, net.x, net.y, net.c, net.dp, net.mp
@@ -274,13 +274,20 @@
     small = [
         pltpu.make_async_copy(src, dst, own_sem.at[len(copies) + i])
         for i, (src, dst) in enumerate(
-            ((qkv_in, QIN), (out_in, OIN), (master, MIN), (gain_one, GIN.at[0]), (gain_two, GIN.at[1]))
+            ((qkv_in, QIN), (out_in, OIN), (master, MIN), (gain_one, GIN.at[0]), (gain_two, GIN.at[1]),
+             (lengths_in, lengths), (tasks_in, tasks))
         )
     ]
     for copy in small:
         copy.start()
     patch_copy.start()
     cot_copy.start()
+    moments = [
+        pltpu.make_async_copy(first_moment, FIRST, local_sem.at[2]),
+        pltpu.make_async_copy(second_moment, SECOND, local_sem.at[3]),
+    ]
+    for copy in moments:
+        copy.start()
     for copy in small:
         copy.wait()
 
@@ -329,10 +336,14 @@
     def place_rows():
         patch_copy.wait()
         cot_copy.wait()
+        for copy in moments:
+            copy.wait()
         for b in range(IMGS):
             RES[b, LEAD:ROWS, :] = PIN[:, b, :].astype(F32)
 
     task_rows = lax.broadcasted_iota(jnp.int32, (TASKS, 1), 0)
+
+    columns = lax.broadcasted_iota(jnp.int32, (TASKS, 128), 1)
 
     def pick(d, _):
         dd, mm = d // 4, d % 4
@@ -347,12 +358,13 @@
         base = PART - half
         for b in range(IMGS):
             which = high[0:1, base + b : base + b + 1]
-            ONEHOT[d, b] = (
-                lax.broadcasted_iota(jnp.int32, (TASKS, 128), 0).astype(F32) == which
-            ).astype(F32)
+            hot = (lax.broadcasted_iota(jnp.int32, (TASKS, 128), 0).astype(F32) == which).astype(F32)
+            for h in range(2):
+                ONEHOT[h] += jnp.where(columns == 2 * IMGS * d + 2 * b + h, hot, 0.0)
         return 0
 
     def place_prompts():
+        ONEHOT[...] = jnp.zeros_like(ONEHOT)
         lax.fori_loop(0, NDEV, pick, 0)
         wide = lax.broadcasted_iota(jnp.int32, (4, D), 1)
         for r in range(25):
@@ -533,17 +545,20 @@
             part = grad[count * i : count * (i + 1)]
             GACC[b, first:last] = G2[b, first:last] + norm_back(NRM1[b, first:last], SC1[b, first:last], g1, part)
 
-    def swap(k, src, dst, sems):
-        to_dp, to_mp = (dp + k // 4) & 7, (mp + k) & 3
-        other = to_dp * 4 + to_mp
-        pltpu.make_async_remote_copy(
-            src_ref=src(other),
-            dst_ref=dst,
-            send_sem=all_sem.at[sems],
-            recv_sem=all_sem.at[sems + 1],
-            device_id=(to_dp, to_mp),
-            device_id_type=MESH,
-        ).start()
+    def to_others(src, dst, sems):
+        for step in (4, 5, 3, 6, 2, 7, 1, 0):
+            to_dp = (dp + step) & 7
+            for turn in range(4):
+                if step or turn:
+                    to_mp = (mp + turn) & 3
+                    pltpu.make_async_remote_copy(
+                        src_ref=src(to_dp * 4 + to_mp),
+                        dst_ref=dst,
+                        send_sem=all_sem.at[sems],
+                        recv_sem=all_sem.at[sems + 1],
+                        device_id=(to_dp, to_mp),
+                        device_id_type=MESH,
+                    ).start()
 
     wide = lax.broadcasted_iota(jnp.int32, (4, PADP), 1)
 
@@ -567,8 +582,7 @@
                     [msg[2 * rep + b : 2 * rep + b + 1, half * h : half * h + half] for b in range(IMGS) for h in range(2)],
                     axis=0,
                 )
-        for k in range(1, NDEV):
-            swap(k, lambda other: SEND.at[other], RECV.at[device], 0)
+        to_others(lambda other: SEND.at[other], RECV.at[device], 0)
         RECV[pl.ds(device, 1)] = SEND[pl.ds(device, 1)]
 
     def others(ref):
@@ -593,16 +607,8 @@
 
     wait_all(RECV, 1)
 
-    def add(s, acc):
-        rows = RECV[s].astype(F32)
-        low, high = acc
-        for b in range(IMGS):
-            hot = jnp.concatenate([ONEHOT[s, b]] * (half // 128), axis=1)
-            low, high = low + hot * rows[2 * b : 2 * b + 1], high + hot * rows[2 * b + 1 : 2 * b + 2]
-        return low, high
-
-    acc = (jnp.zeros((TASKS, half), F32), jnp.zeros((TASKS, half), F32))
-    acc = lax.fori_loop(0, NDEV, add, acc, unroll=8)
+    came = RECV[...].reshape(2 * IMGS * NDEV, half)
+    acc = [nn(ONEHOT[h].astype(BF16), came) for h in range(2)]
     square = total(acc[0] * acc[0]) + total(acc[1] * acc[1])
     lane = lax.broadcasted_iota(jnp.int32, (1, 128), 1)
     count = (limits[0] + limits[1]).astype(F32)
@@ -611,8 +617,7 @@
         stats = jnp.where(lane == i, v, stats)
     STSUM[...] = stats
     SREC[pl.ds(device, 1)] = stats[None]
-    for k in range(1, NDEV):
-        swap(k, lambda other: STSUM, SREC.at[device], 2)
+    to_others(lambda other: STSUM, SREC.at[device], 2)
 
     out_task[...] = jnp.concatenate(acc, axis=1)[:, 0:PART]
     for b in range(IMGS):
@@ -667,16 +672,17 @@
     smem = pl.BlockSpec(memory_space=pltpu.SMEM)
     anywhere = pl.BlockSpec(memory_space=pl.ANY)
     V = pltpu.VMEM
-    block, patch, task, stats = pl.pallas_call(
+    block, patch, *states = pl.pallas_call(
         layer_kernel,
         out_shape=[
             V((IMGS, ROWS, D), BF16),
             V((PATCH, IMGS, D), BF16),
             V((TASKS, PART), F32),
             V((1, 128), F32),
-        ],
-        in_specs=[anywhere, smem, smem] + [anywhere] * 8,
-        out_specs=[vmem] * 4,
+        ]
+        + [V((TASKS, PART), F32)] * 3,
+        in_specs=[anywhere] * 13,
+        out_specs=[vmem] * 7,
         scratch_shapes=[
             V((1, 2, 8, 16, PADP), BF16),
             V((1, 2, 8, 96, 2 * D), BF16),
@@ -710,15 +716,16 @@
             V((PATCH, IMGS, D), BF16),
             V((NDEV, 2 * IMGS, PADP // 2), BF16),
             V((NDEV, 2 * IMGS, PADP // 2), BF16),
-            V((NDEV, IMGS, TASKS, 128), F32),
+            V((2, TASKS, 128), F32),
             V((NDEV, 1, 128), F32),
             V((1, 128), F32),
             V((3, 96, 192), BF16),
             V((192, 96), BF16),
-            V((TASKS, PART), F32),
             V((2, D), F32),
-            pltpu.SemaphoreType.DMA((5 + len(DOWNS) + len(UPS),)),
-            pltpu.SemaphoreType.DMA((2,)),
+            pltpu.SMEM((IMGS,), jnp.int32),
+            pltpu.SMEM((1, IMGS), jnp.int32),
+            pltpu.SemaphoreType.DMA((7 + len(DOWNS) + len(UPS),)),
+            pltpu.SemaphoreType.DMA((4,)),
             pltpu.SemaphoreType.DMA((6 * (2 + len(DOWNS) + len(UPS)),)),
             pltpu.SemaphoreType.DMA((10 + 18 * (1 + len(DOWNS) + len(UPS)),)),
             pltpu.SemaphoreType.DMA((4,)),
@@ -727,7 +734,7 @@
             collective_id=0, has_side_effects=True, vmem_limit_bytes=58 << 20
         ),
     )(
-        patches.transpose(1, 0, 2), lengths, tasks.T, prompt_master, gain_one, gain_two,
+        patches.transpose(1, 0, 2), lengths, tasks.T, prompt_master, first_moment, second_moment, gain_one, gain_two,
         w_qkv.transpose(1, 0, 2), w_out, w_up, w_down.T, cotangent,
     )
     state = jax.ShapeDtypeStruct((TASKS, PART), F32)
@@ -748,9 +755,7 @@
         in_specs=[vmem] * 7,
         out_specs=[vmem] * 5 + [smem] * 2 + [anywhere] * 2,
         scratch_shapes=[pltpu.SemaphoreType.DMA((2,))],
-    )(
-        keep_near(task), keep_near(stats), prompt_master, first_moment, second_moment, keep_near(block), keep_near(patch),
-    )
+    )(*(keep_near(v) for v in (*states, block, patch)))
     return (
         block_out, patch_out.transpose(1, 0, 2), grad, norm.reshape(()), first, second, master, copy, rms,
     )

time: 91 us -> 88.5 us (0.973)
  Pallas kernels: 89.9 us -> 87.5 us
    pallas_call x1, Pallas kernels: 87.3 us -> 85.7 us  [fast_body(): pl.pallas_call(layer_kernel, out_shape=[V((IMGS, ROWS, D), BF16), V((PATC...]
where the time goes in v5:
time: 88.5 us; the launch traced here: 88.3 us
  Pallas kernels  87.5 us (99%)
    pallas_call x1, Pallas kernels, fast_body(): pl.pallas_call(layer_kernel, out_shape=[V((IMGS, ROWS, D), BF16), V((PATC...  85.7 us
    pallas_call x1, Pallas kernels, fast_body(): pl.pallas_call(update_kernel, out_shape=[state] * 4 + [jax.ShapeDtypeStru...  1.78 us

profile of v5, /device:TPU:0, one launch (start us, length us, event | category | flops | bytes accessed | tf_op | source)
XLA Modules:
  0.0 88.3 jit_solution(13770145853776698923)
XLA Ops:
  0.6 85.7 %shard_map.196 = (bf16[2,256,768]{2,1,0:T(8,128)(2,1)S(1)}, bf16[206,2,768]{2,1,0:T(2,128)(2,1)S(1)}, f32[8,1200]{1,0:T(8,128)S(1)}, f32[1,128]{1,0:T(1,128)S(1)...) custom-call(bf16[206,2,768]{2,1,0:T(2,128)(2,1)} %bitcast.6, s32[2]{0:T(128)} %lengths_in.1, ...), custom_call_target="tpu_custom_call" | custom-call | tf_op jit(solution)/shard_map/pallas_call | solution.py:675
  86.4 1.8 %shard_map.197 = (f32[8,1200]{1,0:T(8,128)}, f32[8,1200]{1,0:T(8,128)}, f32[8,1200]{1,0:T(8,128)}, f32[8,1200]{1,0:T(8,128)}, bf16[8,1200]{1,0:T(8,128)(2,1)}, /...) custom-call(f32[8,1200]{1,0:T(8,128)S(1)} %get-tuple-element.25.task_grad, ...), custom_call_target="tpu_custom_call" | custom-call | tf_op jit(solution)/shard_map/pallas_call | solution.py:745

commit v6 on v5

--- a/solution.py
+++ b/solution.py
@@ -460,7 +460,15 @@
             ACT[yy, :, here] = (up * cumul).astype(BF16)
             GU[yy, :, here] = (back * (cumul + up * density)).astype(BF16)
 
-    def add_units(i, yy):
+    def add_grad(i, yy):
+        w = UPS[i]
+        grad = nt(GU[yy, :, 0 : 2 * w], weight(GUS[i].at[0, yy], 0, 0, 2 * w, w)).reshape(IMGS, ROWS, D)
+        if i == 0 and yy == 0:
+            GACC[...] = grad
+        else:
+            GACC[...] += grad
+
+    def add_mlp(i, yy):
         w, first = UPS[i], sum(UPS[:i])
         d = max(d for d in range(len(DOWNS)) if sum(DOWNS[:d]) <= first)
         inside = first - sum(DOWNS[:d])
@@ -471,14 +479,16 @@
                 nt(ACT[yy, :, w * core : w * (core + 1)], weight(GDS[d].at[0, yy], core, inside, w, DOWNS[d]))
                 for core in range(2)
             )
-        grad = nt(GU[yy, :, 0 : 2 * w], weight(GUS[i].at[0, yy], 0, 0, 2 * w, w))
-        mlp, grad = mlp.reshape(IMGS, ROWS, D), grad.reshape(IMGS, ROWS, D)
+        mlp = mlp.reshape(IMGS, ROWS, D)
         if i == 0 and yy == 0:
             MACC[...] = mlp
-            GACC[...] = grad
         else:
             MACC[...] += mlp
-            GACC[...] += grad
+
+    def add_units(i, yy):
+        add_grad(i, yy)
+        if i < len(UPS) - 1:
+            add_mlp(i, yy)
 
     steps = [place_rows, place_prompts, norm_one]
     steps += [functools.partial(project, m) for m in range(4)]
@@ -499,13 +509,10 @@
         G2[b] = g
         G2B[b] = g.astype(BF16)
 
-    def context_back(m, _):
+    for m in range(4):
         cols = pl.ds(pl.multiple_of((m % 2) * D + 512, 128), 256)
         w = GA[0, m // 2, :, :, cols].reshape(D, 256)
         DC[m] = nn(G2B[...].reshape(IMGS * ROWS, D), w).astype(BF16).reshape(IMGS, ROWS, 256)
-        return 0
-
-    lax.fori_loop(0, 4, context_back, 0, unroll=4)
 
     def attend_back(b):
         tiles, grad_probs, grad_scores = [], [], []
@@ -598,6 +605,8 @@
     to_owners()
 
     grad_rows((0, 1), some, ROWS)
+    for yy in range(2):
+        add_mlp(len(UPS) - 1, yy)
     for b in range(IMGS):
         mlp = MACC[b]
         block = RES2[b] + mlp

time: 88.5 us -> 88 us (level)
  no operation moved by 1% of the time
where the time goes in v6:
time: 88 us; the launch traced here: 87.8 us
  Pallas kernels  87 us (99%)
    pallas_call x1, Pallas kernels, fast_body(): pl.pallas_call(layer_kernel, out_shape=[V((IMGS, ROWS, D), BF16), V((PATC...  85.2 us
    pallas_call x1, Pallas kernels, fast_body(): pl.pallas_call(update_kernel, out_shape=[state] * 4 + [jax.ShapeDtypeStru...  1.78 us

profile of v6, /device:TPU:0, one launch (start us, length us, event | category | flops | bytes accessed | tf_op | source)
XLA Modules:
  0.0 87.8 jit_solution(4087061566554430441)
XLA Ops:
  0.6 85.2 %shard_map.196 = (bf16[2,256,768]{2,1,0:T(8,128)(2,1)S(1)}, bf16[206,2,768]{2,1,0:T(2,128)(2,1)S(1)}, f32[8,1200]{1,0:T(8,128)S(1)}, f32[1,128]{1,0:T(1,128)S(1)...) custom-call(bf16[206,2,768]{2,1,0:T(2,128)(2,1)} %bitcast.6, s32[2]{0:T(128)} %lengths_in.1, ...), custom_call_target="tpu_custom_call" | custom-call | tf_op jit(solution)/shard_map/pallas_call | solution.py:684
  85.8 1.8 %shard_map.197 = (f32[8,1200]{1,0:T(8,128)}, f32[8,1200]{1,0:T(8,128)}, f32[8,1200]{1,0:T(8,128)}, f32[8,1200]{1,0:T(8,128)}, bf16[8,1200]{1,0:T(8,128)(2,1)}, /...) custom-call(f32[8,1200]{1,0:T(8,128)S(1)} %get-tuple-element.25.task_grad, ...), custom_call_target="tpu_custom_call" | custom-call | tf_op jit(solution)/shard_map/pallas_call | solution.py:754

commit v7 on v6

--- a/solution.py
+++ b/solution.py
@@ -88,11 +88,11 @@
 def gather_events(net, G, W, split):
     z, x, y, c = net.z, net.x, net.y, net.c
     r1, r2, r3, rows = split
-    some = 4 if r3 > r1 else 0
+    some = 1 if r3 > r1 else 0
     f_sem = net.recvs
-    zs_sem, zp_sem, m_sem = f_sem + 1, f_sem + 1 + some, f_sem + 5 + some
-    l_sem, c_sem = f_sem + 5 + 2 * some, f_sem + 9 + 2 * some
-    net.recvs = c_sem + 1
+    zp_sem, l_sem = f_sem + 1, f_sem + 4
+    c_sem, zs_sem, m_sem = f_sem + 8, f_sem + 9, f_sem + 12
+    net.recvs = f_sem + 9 + 7 * some
     start_sent, single_sent, pair_sent, middle_sent, last_sent, core_sent = range(net.sends, net.sends + 6)
     net.sends += 6
     every = slice(None)
@@ -120,6 +120,9 @@
             pl.when(z >= k)(lambda: f(z - k, "u", z < 3))
             pl.when(z + k <= 3)(lambda: f(z + k, "d", z > 0))
 
+    def along(sem, p, zz):
+        return sem + p - (p > zz).astype(jnp.int32)
+
     def middle(p):
         send("x", y, one(p), r1, r2, middle_sent, m_sem + p)
         send("y", y, one(p), r2, r3, middle_sent, m_sem + p)
@@ -128,13 +131,14 @@
         send("x", y, one(z), 0, r1, start_sent, f_sem)
         send("y", y, one(z), r3, rows, start_sent, f_sem)
         if r3 > r1:
-            pl.when(z < 3)(lambda: send("u", y, one(z), r1, r3, single_sent, zs_sem + z))
-            pl.when(z > 0)(lambda: send("d", y, one(z), r1, r3, single_sent, zs_sem + z))
+            pl.when(z < 3)(lambda: send("u", y, one(z), r1, r3, single_sent, along(zs_sem, z, z + 1)))
+            pl.when(z > 0)(lambda: send("d", y, one(z), r1, r3, single_sent, along(zs_sem, z, z - 1)))
             middle(z)
 
     def pair(way, p):
-        send(way, y, two(p), 0, r1, pair_sent, zp_sem + p)
-        send(way, every, one(p), r3, rows, pair_sent, zp_sem + p)
+        landed = along(zp_sem, p, z + 1 if way == "u" else z - 1)
+        send(way, y, two(p), 0, r1, pair_sent, landed)
+        send(way, every, one(p), r3, rows, pair_sent, landed)
 
     def first_hop():
         net.recv(V(y, one(z), 0, ends), f_sem)
@@ -143,16 +147,17 @@
 
     def single_hop(k):
         def hop(p, way, more):
-            net.recv(V(y, one(p), r1, r3), zs_sem + p)
+            net.recv(V(y, one(p), r1, r3), along(zs_sem, p, z))
             if k < 3:
-                pl.when(more)(lambda: send(way, y, one(p), r1, r3, single_sent, zs_sem + p))
+                on = z + 1 if way == "u" else z - 1
+                pl.when(more)(lambda: send(way, y, one(p), r1, r3, single_sent, along(zs_sem, p, on)))
             middle(p)
 
         sides(k, hop)
 
     def pair_hop(k):
         def hop(p, way, more):
-            net.recv(V(y, two(p), 0, ends), zp_sem + p)
+            net.recv(V(y, two(p), 0, ends), along(zp_sem, p, z))
             if k < 3:
                 pl.when(more)(lambda: pair(way, p))
 
@@ -185,7 +190,7 @@
         if r3 > r1:
             net.wait_sent(V(y, pl.ds(0, 4), r1, r3), middle_sent)
 
-        def along(count):
+        def chain(count):
             if r3 > r1:
                 net.wait_sent(V(y, pl.ds(0, count), r1, r3), single_sent)
             total = 2 * ends * count
@@ -195,8 +200,8 @@
             net.wait_sent(V(y if yy == 1 else every, pl.ds(0, blocks), 0, total // (yy * blocks)), pair_sent)
 
         inner = jnp.logical_and(z > 0, z < 3)
-        pl.when(inner)(lambda: along(5))
-        pl.when(jnp.logical_not(inner))(lambda: along(1))
+        pl.when(inner)(lambda: chain(5))
+        pl.when(jnp.logical_not(inner))(lambda: chain(1))
 
     kinds = (start, first_hop, single_hop, pair_hop, last_hop, to_core, from_core)
     return [f if i < 2 else functools.partial(f, k) for i, f in enumerate(kinds) for k in range(4)], finish
@@ -552,9 +557,9 @@
             part = grad[count * i : count * (i + 1)]
             GACC[b, first:last] = G2[b, first:last] + norm_back(NRM1[b, first:last], SC1[b, first:last], g1, part)
 
-    def to_others(src, dst, sems):
-        for step in (4, 5, 3, 6, 2, 7, 1, 0):
-            to_dp = (dp + step) & 7
+    def to_others(src, dst, sems, mirror=False):
+        for step in (7, 6, 5, 4, 3, 2, 1, 0) if mirror else (4, 5, 3, 6, 2, 7, 1, 0):
+            to_dp = dp ^ step if mirror else (dp + step) & 7
             for turn in range(4):
                 if step or turn:
                     to_mp = (mp + turn) & 3
@@ -626,7 +631,7 @@
         stats = jnp.where(lane == i, v, stats)
     STSUM[...] = stats
     SREC[pl.ds(device, 1)] = stats[None]
-    to_others(lambda other: STSUM, SREC.at[device], 2)
+    to_others(lambda other: STSUM, SREC.at[device], 2, mirror=True)
 
     out_task[...] = jnp.concatenate(acc, axis=1)[:, 0:PART]
     for b in range(IMGS):
@@ -736,7 +741,7 @@
             pltpu.SemaphoreType.DMA((7 + len(DOWNS) + len(UPS),)),
             pltpu.SemaphoreType.DMA((4,)),
             pltpu.SemaphoreType.DMA((6 * (2 + len(DOWNS) + len(UPS)),)),
-            pltpu.SemaphoreType.DMA((10 + 18 * (1 + len(DOWNS) + len(UPS)),)),
+            pltpu.SemaphoreType.DMA((9 + 16 * (1 + len(DOWNS) + len(UPS)),)),
             pltpu.SemaphoreType.DMA((4,)),
         ],
         compiler_params=pltpu.CompilerParams(

time: 88 us -> 87.7 us (level)
  no operation moved by 1% of the time
where the time goes in v7:
time: 87.7 us; the launch traced here: 87.5 us
  Pallas kernels  86.7 us (99%)
    pallas_call x1, Pallas kernels, fast_body(): pl.pallas_call(layer_kernel, out_shape=[V((IMGS, ROWS, D), BF16), V((PATC...  84.9 us
    pallas_call x1, Pallas kernels, fast_body(): pl.pallas_call(update_kernel, out_shape=[state] * 4 + [jax.ShapeDtypeStru...  1.78 us

profile of v7, /device:TPU:0, one launch (start us, length us, event | category | flops | bytes accessed | tf_op | source)
XLA Modules:
  0.0 87.5 jit_solution(3161917408429677512)
XLA Ops:
  0.6 84.9 %shard_map.196 = (bf16[2,256,768]{2,1,0:T(8,128)(2,1)S(1)}, bf16[206,2,768]{2,1,0:T(2,128)(2,1)S(1)}, f32[8,1200]{1,0:T(8,128)S(1)}, f32[1,128]{1,0:T(1,128)S(1)...) custom-call(bf16[206,2,768]{2,1,0:T(2,128)(2,1)} %bitcast.6, s32[2]{0:T(128)} %lengths_in.1, ...), custom_call_target="tpu_custom_call" | custom-call | tf_op jit(solution)/shard_map/pallas_call | solution.py:689
  85.6 1.8 %shard_map.197 = (f32[8,1200]{1,0:T(8,128)}, f32[8,1200]{1,0:T(8,128)}, f32[8,1200]{1,0:T(8,128)}, f32[8,1200]{1,0:T(8,128)}, bf16[8,1200]{1,0:T(8,128)(2,1)}, /...) custom-call(f32[8,1200]{1,0:T(8,128)S(1)} %get-tuple-element.25.task_grad, ...), custom_call_target="tpu_custom_call" | custom-call | tf_op jit(solution)/shard_map/pallas_call | solution.py:759
